TPU v7x, 256 devices: a whole 4x4x8 slice. The times are simulated.
256 devices in a mesh: ax: 16 (over y_hi, x, core), az: 16 (over z, y_lo).
Axes of the slice: x: 4, y: 4 (y_hi: 2, y_lo: 2; y = y_hi * 2 + y_lo), z: 8, core: 2. Of those that a mesh axis runs over, the one named last changes fastest.
Arguments:
- adjoint: float32 [5, 2, 256, 128, 128], P(None, None, 'ax', 'az'), may hold values from -6 to 6
- mean_flow: float32 [3, 256, 128, 128], P(None, 'ax', 'az'), may hold values from 0.5 to 1.5
- forcing: float32 [2, 256, 128, 128], P(None, 'ax', 'az'), may hold values from -6 to 6
- tke: float32 [256, 128, 128], P('ax', 'az'), may hold values from 0.03 to 0.3
- half_width: int32 [256, 128, 128], P('ax', 'az'), may hold values from 2 to 16
- start: int32 [1], replicated, may hold values from 0 to 1792
Outputs:
- green: float32 [5, 2, 256, 128, 128], P(None, None, 'ax', 'az')
- intensity: float32 [256, 128, 128], P('ax', 'az')
All inputs are finite; a program needn't handle non-finite values.
Results may differ from a plain program's by a relative error of at most 0.00002.
Values sent between devices are 32-bit elements; how exact they have to be, the bound alone decides.
A program may use at most 64 MiB of HBM per device.

v0:
```python
import math

import jax
import jax.numpy as jnp
from jax import lax
from jax.sharding import PartitionSpec as P

SEP = 16
ITERS = 2
NAXIAL = 2048


FREQUENCY = 0.7
SECTION_WEIGHTS = (1.0 / 3.0, 0.5, 1.0)


def extended(cells, sides, width, closed):
    for axis, dim in sides:
        count = lax.axis_size(axis)
        ends = count if closed else count - 1
        head = lax.slice_in_dim(cells, 0, width, axis=dim)
        tail = lax.slice_in_dim(cells, cells.shape[dim] - width, cells.shape[dim], axis=dim)
        cells = jnp.concatenate(
            [
                lax.ppermute(tail, axis, [(i, (i + 1) % count) for i in range(ends)]),
                cells,
                lax.ppermute(head, axis, [((i + 1) % count, i) for i in range(ends)]),
            ],
            axis=dim,
        )
    return cells


def shifted_2(value, axis, steps):
    count = lax.axis_size(axis)
    pairs = [(source, (source + steps) % count) for source in range(count)]
    return lax.ppermute(value, axis, pairs)


def coefficients(mean_flow):
    return jnp.stack([mean_flow[0], mean_flow[1], mean_flow[1] * mean_flow[2], 1.0 / mean_flow[1]])


def axial_flux(state, coeffs):
    speed = coeffs[0][None]
    density = coeffs[1][None]
    stiff = coeffs[2][None]
    inverse = coeffs[3][None]
    return jnp.stack(
        [
            speed * state[0],
            density * state[0] + speed * state[1] + stiff * state[4],
            speed * state[2],
            speed * state[3],
            state[1] * inverse + speed * state[4],
        ]
    )


def shared_flux(state, coeffs):
    return coeffs[1][None] * state[0] + coeffs[2][None] * state[4]


def per_device(adjoint, mean_flow, forcing, tke, half_width, start):
    cells_x = adjoint.shape[2]
    cells_t = adjoint.shape[3]
    radial_cells = adjoint.shape[4]
    sectors = lax.axis_size("az")
    azimuth_step = 2 * math.pi / (cells_t * sectors)
    radius = jnp.arange(radial_cells, dtype=jnp.float32) + 0.5
    tstep = 0.8 / (2.0 + 1.0 / (radius * azimuth_step))
    offset = lax.axis_index("ax") * cells_x + start[0]
    axial_pos = (offset + jnp.arange(cells_x, dtype=jnp.int32)).astype(jnp.float32)
    damping = (0.5 * (axial_pos + 0.5) / NAXIAL)[:, None, None]
    coeffs = coefficients(mean_flow)
    coeffs_x = extended(coeffs, (("ax", 1),), 1, False)
    coeffs_t = extended(coeffs, (("az", 2),), 1, True)
    state = adjoint
    for outer in range(ITERS):
        base = state
        for section_weight in SECTION_WEIGHTS:
            state_x = extended(state, (("ax", 2),), 1, False)
            flux_x = axial_flux(state_x, coeffs_x)
            state_t = extended(state, (("az", 3),), 1, True)
            shared_t = shared_flux(state_t, coeffs_t)
            wrapped = jnp.stack([shared_t, state_t[3] * coeffs_t[3][None]])
            shared = shared_t[:, :, 1:-1]
            radial = jnp.stack([shared, state[2] * coeffs[3][None]])
            mirrored = shifted_2(radial[..., 0], "az", sectors // 2)
            scaled = radius * radial
            padded = jnp.concatenate(
                [0.5 * mirrored[..., None], scaled, jnp.zeros_like(scaled[..., :1])], axis=-1
            )
            along_x = (flux_x[:, :, 2:] - flux_x[:, :, :-2]) * 0.5
            along_t = (wrapped[:, :, :, 2:] - wrapped[:, :, :, :-2]) * (
                0.5 / (azimuth_step * radius)
            )
            along_r = (padded[..., 2:] - padded[..., :-2]) * (0.5 / radius)
            components = jnp.stack(
                [
                    along_x[0],
                    along_x[1],
                    along_x[2] + along_r[0],
                    along_x[3] + along_t[0],
                    along_x[4] + along_r[1] + along_t[1],
                ]
            )
            right_summed = (
                components
                - damping * state
                + FREQUENCY * jnp.stack([state[:, 1], -state[:, 0]], axis=1)
            )
            state = base + section_weight * (tstep * right_summed.at[4].add(forcing))
    pressure = state[4]
    widened = extended(pressure, (("ax", 1),), SEP, False)
    length = half_width.astype(jnp.float32)
    inverse = 1.0 / (length * length)
    summed = jnp.zeros(pressure.shape[1:], jnp.float32)
    for shift_by in range(-SEP, SEP + 1):
        shifted = widened[:, SEP + shift_by : SEP + shift_by + cells_x]
        weight = jnp.exp(-(shift_by * shift_by) * inverse)
        summed = summed + weight * (pressure[0] * shifted[0] + pressure[1] * shifted[1])
    return (state, tke * summed)


def solution(mesh):
    return jax.shard_map(
        per_device,
        mesh=mesh,
        in_specs=(
            P(None, None, "ax", "az", None),
            P(None, "ax", "az", None),
            P(None, "ax", "az", None),
            P("ax", "az", None),
            P("ax", "az", None),
            P(),
        ),
        out_specs=(P(None, None, "ax", "az", None), P("ax", "az", None)),
        check_vma=False,
    )
```

profile of v0, /device:TPU:7, one launch (start us, length us, event | category | flops | bytes accessed | tf_op | source)
XLA Modules:
  0.0 216.8 jit_solution(5755964057202336975)
XLA Ops:
  1.7 5.3 %collective-permute-start = (f32[4,1,8,128]{3,2,1,0:T(8,128)S(1)}, f32[4,1,8,128]{3,2,1,0:T(8,128)S(1)}, u32[]{:S(2)}, u32[]{:S(2)}) collective-permute-start(f32[4,1,8,128]{3,2,1,0:T(8,128)S(1)} %get-tuple-element.165), channel_id=1, source_target_pairs={{0,16},{16,32},{32,48},{48,64},{64,80},{80,96},{96,112},{112,128},... | collective-permute-start | bytes 49160 | tf_op jit(solution)/shard_map/ppermute | solution.py:25
  7.0 1.9 collective-permute-start.1
  8.9 7.3 %collective-permute-start.2 = (f32[5,2,1,8,128]{4,3,2,1,0:T(8,128)S(1)}, f32[5,2,1,8,128]{4,3,2,1,0:T(8,128)S(1)}, u32[]{:S(2)}, u32[]{:S(2)}) collective-permute-start(f32[5,2,1,8,128]{4,3,2,1,0:T(8,128)S(1)} %get-tuple-element.155), channel_id=1, source_target_pairs={{0,16},{16,32},{32,48},{48,64},{64,80},{80,96},{96,112},{112,128},... | collective-permute-start | bytes 122888 | tf_op jit(solution)/shard_map/ppermute | solution.py:25
  16.2 1.9 collective-permute-start.3
  19.6 5.4 %collective-permute-start.5 = (f32[4,16,1,128]{3,2,1,0:T(1,128)S(1)}, f32[4,16,1,128]{3,2,1,0:T(1,128)S(1)}, u32[]{:S(2)}, u32[]{:S(2)}) collective-permute-start(f32[4,16,1,128]{3,2,1,0:T(1,128)S(1)} %get-tuple-element.168), channel_id=1, source_target_pairs={{1,0},{2,1},{3,2},{4,3},{5,4},{6,5},{7,6},{8,7},{9,8},{10,9},{11,1... | collective-permute-start | bytes 98312 | tf_op jit(solution)/shard_map/ppermute | solution.py:27
  25.2 3.4 %collective-permute-start.7 = (f32[5,2,16,1,128]{4,2,3,1,0:T(8,128)S(1)}, f32[5,2,16,1,128]{4,2,3,1,0:T(8,128)S(1)}, u32[]{:S(2)}, u32[]{:S(2)}) collective-permute-start(f32[5,2,16,1,128]{4,2,3,1,0:T(8,128)S(1)} %bitcast.701), channel_id=1, source_target_pairs={{1,0},{2,1},{3,2},{4,3},{5,4},{6,5},{7,6},{8,7},{9,8},{10,9},{11,1... | collective-permute-start | bytes 245768 | tf_op jit(solution)/shard_map/ppermute | solution.py:27
  33.2 4.8 %collective-permute-start.8 = (f32[2,2,16,8]{2,3,1,0:T(8,128)S(1)}, f32[2,2,16,8]{2,3,1,0:T(8,128)S(1)}, u32[]{:S(2)}, u32[]{:S(2)}) collective-permute-start(f32[2,2,16,8]{2,3,1,0:T(8,128)S(1)} %bitcast.718), channel_id=1, source_target_pairs={{0,8},{1,9},{2,10},{3,11},{4,12},{5,13},{6,14},{7,15},{8,0},{9,1},... | collective-permute-start | bytes 6152 | tf_op jit(solution)/shard_map/ppermute | solution.py:37
  46.8 10.4 %collective-permute-start.9 = (f32[5,2,1,8,128]{4,3,2,1,0:T(8,128)S(1)}, f32[5,2,1,8,128]{4,3,2,1,0:T(8,128)S(1)}, u32[]{:S(2)}, u32[]{:S(2)}) collective-permute-start(f32[5,2,1,8,128]{4,3,2,1,0:T(8,128)S(1)} %get-tuple-element.148), channel_id=1, source_target_pairs={{0,16},{16,32},{32,48},{48,64},{64,80},{80,96},{96,112},{112,128},... | collective-permute-start | bytes 122888 | tf_op jit(solution)/shard_map/ppermute | solution.py:25
  57.4 3.6 %collective-permute-start.12 = (f32[5,2,16,1,128]{4,2,3,1,0:T(8,128)S(1)}, f32[5,2,16,1,128]{4,2,3,1,0:T(8,128)S(1)}, u32[]{:S(2)}, u32[]{:S(2)}) collective-permute-start(f32[5,2,16,1,128]{4,2,3,1,0:T(8,128)S(1)} %bitcast.705), channel_id=1, source_target_pairs={{1,0},{2,1},{3,2},{4,3},{5,4},{6,5},{7,6},{8,7},{9,8},{10,9},{11,1... | collective-permute-start | bytes 245768 | tf_op jit(solution)/shard_map/ppermute | solution.py:27
  66.5 4.5 %collective-permute-start.13 = (f32[2,2,16,8]{2,3,1,0:T(8,128)S(1)}, f32[2,2,16,8]{2,3,1,0:T(8,128)S(1)}, u32[]{:S(2)}, u32[]{:S(2)}) collective-permute-start(f32[2,2,16,8]{2,3,1,0:T(8,128)S(1)} %bitcast.714), channel_id=1, source_target_pairs={{0,8},{1,9},{2,10},{3,11},{4,12},{5,13},{6,14},{7,15},{8,0},{9,1},... | collective-permute-start | bytes 6152 | tf_op jit(solution)/shard_map/ppermute | solution.py:37
  77.6 5.6 %collective-permute-start.14 = (f32[5,2,1,8,128]{4,3,2,1,0:T(8,128)S(1)}, f32[5,2,1,8,128]{4,3,2,1,0:T(8,128)S(1)}, u32[]{:S(2)}, u32[]{:S(2)}) collective-permute-start(f32[5,2,1,8,128]{4,3,2,1,0:T(8,128)S(1)} %get-tuple-element.142), channel_id=1, source_target_pairs={{0,16},{16,32},{32,48},{48,64},{64,80},{80,96},{96,112},{112,128},... | collective-permute-start | bytes 122888 | tf_op jit(solution)/shard_map/ppermute | solution.py:25
  83.2 1.9 collective-permute-start.15
  85.2 3.6 %collective-permute-start.17 = (f32[5,2,16,1,128]{4,2,3,1,0:T(8,128)S(1)}, f32[5,2,16,1,128]{4,2,3,1,0:T(8,128)S(1)}, u32[]{:S(2)}, u32[]{:S(2)}) collective-permute-start(f32[5,2,16,1,128]{4,2,3,1,0:T(8,128)S(1)} %bitcast.706), channel_id=1, source_target_pairs={{1,0},{2,1},{3,2},{4,3},{5,4},{6,5},{7,6},{8,7},{9,8},{10,9},{11,1... | collective-permute-start | bytes 245768 | tf_op jit(solution)/shard_map/ppermute | solution.py:27
  88.8 3.3 %collective-permute-done.15 = f32[5,2,1,8,128]{4,3,2,1,0:T(8,128)S(1)} collective-permute-done((f32[5,2,1,8,128]{4,3,2,1,0:T(8,128)S(1)}, f32[5,2,1,8,128]{4,3,2,1,0:T(8,128)S(1)}, u32[]{:S(2)}, u32[]{:S(2)}) %collective-permute-start.15) | collective-permute-done | bytes 40992 | tf_op jit(solution)/shard_map/ppermute | solution.py:27
  96.8 4.7 %collective-permute-start.18 = (f32[2,2,16,8]{2,3,1,0:T(8,128)S(1)}, f32[2,2,16,8]{2,3,1,0:T(8,128)S(1)}, u32[]{:S(2)}, u32[]{:S(2)}) collective-permute-start(f32[2,2,16,8]{2,3,1,0:T(8,128)S(1)} %bitcast.715), channel_id=1, source_target_pairs={{0,8},{1,9},{2,10},{3,11},{4,12},{5,13},{6,14},{7,15},{8,0},{9,1},... | collective-permute-start | bytes 6152 | tf_op jit(solution)/shard_map/ppermute | solution.py:37
  107.4 7.2 %collective-permute-start.19 = (f32[5,2,1,8,128]{4,3,2,1,0:T(8,128)S(1)}, f32[5,2,1,8,128]{4,3,2,1,0:T(8,128)S(1)}, u32[]{:S(2)}, u32[]{:S(2)}) collective-permute-start(f32[5,2,1,8,128]{4,3,2,1,0:T(8,128)S(1)} %get-tuple-element.136), channel_id=1, source_target_pairs={{0,16},{16,32},{32,48},{48,64},{64,80},{80,96},{96,112},{112,128},... | collective-permute-start | bytes 122888 | tf_op jit(solution)/shard_map/ppermute | solution.py:25
  114.6 1.9 collective-permute-start.20
  116.6 3.6 %collective-permute-start.22 = (f32[5,2,16,1,128]{4,2,3,1,0:T(8,128)S(1)}, f32[5,2,16,1,128]{4,2,3,1,0:T(8,128)S(1)}, u32[]{:S(2)}, u32[]{:S(2)}) collective-permute-start(f32[5,2,16,1,128]{4,2,3,1,0:T(8,128)S(1)} %bitcast.707), channel_id=1, source_target_pairs={{1,0},{2,1},{3,2},{4,3},{5,4},{6,5},{7,6},{8,7},{9,8},{10,9},{11,1... | collective-permute-start | bytes 245768 | tf_op jit(solution)/shard_map/ppermute | solution.py:27
  120.2 3.3 %collective-permute-done.20 = f32[5,2,1,8,128]{4,3,2,1,0:T(8,128)S(1)} collective-permute-done((f32[5,2,1,8,128]{4,3,2,1,0:T(8,128)S(1)}, f32[5,2,1,8,128]{4,3,2,1,0:T(8,128)S(1)}, u32[]{:S(2)}, u32[]{:S(2)}) %collective-permute-start.20) | collective-permute-done | bytes 40992 | tf_op jit(solution)/shard_map/ppermute | solution.py:27
  127.4 4.6 %collective-permute-start.23 = (f32[2,2,16,8]{2,3,1,0:T(8,128)S(1)}, f32[2,2,16,8]{2,3,1,0:T(8,128)S(1)}, u32[]{:S(2)}, u32[]{:S(2)}) collective-permute-start(f32[2,2,16,8]{2,3,1,0:T(8,128)S(1)} %bitcast.716), channel_id=1, source_target_pairs={{0,8},{1,9},{2,10},{3,11},{4,12},{5,13},{6,14},{7,15},{8,0},{9,1},... | collective-permute-start | bytes 6152 | tf_op jit(solution)/shard_map/ppermute | solution.py:37
  137.3 7.1 %collective-permute-start.24 = (f32[5,2,1,8,128]{4,3,2,1,0:T(8,128)S(1)}, f32[5,2,1,8,128]{4,3,2,1,0:T(8,128)S(1)}, u32[]{:S(2)}, u32[]{:S(2)}) collective-permute-start(f32[5,2,1,8,128]{4,3,2,1,0:T(8,128)S(1)} %get-tuple-element.130), channel_id=1, source_target_pairs={{0,16},{16,32},{32,48},{48,64},{64,80},{80,96},{96,112},{112,128},... | collective-permute-start | bytes 122888 | tf_op jit(solution)/shard_map/ppermute | solution.py:25
  146.5 3.6 %collective-permute-start.27 = (f32[5,2,16,1,128]{4,2,3,1,0:T(8,128)S(1)}, f32[5,2,16,1,128]{4,2,3,1,0:T(8,128)S(1)}, u32[]{:S(2)}, u32[]{:S(2)}) collective-permute-start(f32[5,2,16,1,128]{4,2,3,1,0:T(8,128)S(1)} %bitcast.708), channel_id=1, source_target_pairs={{1,0},{2,1},{3,2},{4,3},{5,4},{6,5},{7,6},{8,7},{9,8},{10,9},{11,1... | collective-permute-start | bytes 245768 | tf_op jit(solution)/shard_map/ppermute | solution.py:27
  150.1 3.3 %collective-permute-done.25 = f32[5,2,1,8,128]{4,3,2,1,0:T(8,128)S(1)} collective-permute-done((f32[5,2,1,8,128]{4,3,2,1,0:T(8,128)S(1)}, f32[5,2,1,8,128]{4,3,2,1,0:T(8,128)S(1)}, u32[]{:S(2)}, u32[]{:S(2)}) %collective-permute-start.25) | collective-permute-done | bytes 40992 | tf_op jit(solution)/shard_map/ppermute | solution.py:27
  158.0 4.5 %collective-permute-start.28 = (f32[2,2,16,8]{2,3,1,0:T(8,128)S(1)}, f32[2,2,16,8]{2,3,1,0:T(8,128)S(1)}, u32[]{:S(2)}, u32[]{:S(2)}) collective-permute-start(f32[2,2,16,8]{2,3,1,0:T(8,128)S(1)} %bitcast.717), channel_id=1, source_target_pairs={{0,8},{1,9},{2,10},{3,11},{4,12},{5,13},{6,14},{7,15},{8,0},{9,1},... | collective-permute-start | bytes 6152 | tf_op jit(solution)/shard_map/ppermute | solution.py:37
  169.2 7.3 %collective-permute-start.29 = (f32[5,2,1,8,128]{4,3,2,1,0:T(8,128)S(1)}, f32[5,2,1,8,128]{4,3,2,1,0:T(8,128)S(1)}, u32[]{:S(2)}, u32[]{:S(2)}) collective-permute-start(f32[5,2,1,8,128]{4,3,2,1,0:T(8,128)S(1)} %get-tuple-element.124), channel_id=1, source_target_pairs={{0,16},{16,32},{32,48},{48,64},{64,80},{80,96},{96,112},{112,128},... | collective-permute-start | bytes 122888 | tf_op jit(solution)/shard_map/ppermute | solution.py:25
  178.5 3.6 %collective-permute-start.32 = (f32[5,2,16,1,128]{4,2,3,1,0:T(8,128)S(1)}, f32[5,2,16,1,128]{4,2,3,1,0:T(8,128)S(1)}, u32[]{:S(2)}, u32[]{:S(2)}) collective-permute-start(f32[5,2,16,1,128]{4,2,3,1,0:T(8,128)S(1)} %bitcast.703), channel_id=1, source_target_pairs={{1,0},{2,1},{3,2},{4,3},{5,4},{6,5},{7,6},{8,7},{9,8},{10,9},{11,1... | collective-permute-start | bytes 245768 | tf_op jit(solution)/shard_map/ppermute | solution.py:27
  182.1 3.3 %collective-permute-done.30 = f32[5,2,1,8,128]{4,3,2,1,0:T(8,128)S(1)} collective-permute-done((f32[5,2,1,8,128]{4,3,2,1,0:T(8,128)S(1)}, f32[5,2,1,8,128]{4,3,2,1,0:T(8,128)S(1)}, u32[]{:S(2)}, u32[]{:S(2)}) %collective-permute-start.30) | collective-permute-done | bytes 40992 | tf_op jit(solution)/shard_map/ppermute | solution.py:27
  188.3 4.4 %collective-permute-start.33 = (f32[2,2,16,8]{2,3,1,0:T(8,128)S(1)}, f32[2,2,16,8]{2,3,1,0:T(8,128)S(1)}, u32[]{:S(2)}, u32[]{:S(2)}) collective-permute-start(f32[2,2,16,8]{2,3,1,0:T(8,128)S(1)} %bitcast.713), channel_id=1, source_target_pairs={{0,8},{1,9},{2,10},{3,11},{4,12},{5,13},{6,14},{7,15},{8,0},{9,1},... | collective-permute-start | bytes 6152 | tf_op jit(solution)/shard_map/ppermute | solution.py:37
  192.8 2.1 collective-permute-done.33
  198.5 7.3 %collective-permute-start.34 = (f32[2,16,8,128]{3,2,1,0:T(8,128)S(1)}, f32[2,16,8,128]{3,2,1,0:T(8,128)S(1)}, u32[]{:S(2)}, u32[]{:S(2)}) collective-permute-start(f32[2,16,8,128]{3,2,1,0:T(8,128)S(1)} %slice_bitcast_fusion), channel_id=1, source_target_pairs={{0,16},{16,32},{32,48},{48,64},{64,80},{80,96},{96,112},{112,128},... | collective-permute-start | bytes 393224 | tf_op jit(solution)/shard_map/ppermute | solution.py:25
  205.7 1.9 collective-permute-start.35
  207.7 8.0 %collective-permute-done.35 = f32[2,16,8,128]{3,2,1,0:T(8,128)S(1)} collective-permute-done((f32[2,16,8,128]{3,2,1,0:T(8,128)S(1)}, f32[2,16,8,128]{3,2,1,0:T(8,128)S(1)}, u32[]{:S(2)}, u32[]{:S(2)}) %collective-permute-start.35) | collective-permute-done | bytes 131104 | tf_op jit(solution)/shard_map/ppermute | solution.py:27
  (255 shorter events, 69.8 us)
Async XLA Ops:
  1.7 17.9 %collective-permute-start = (f32[4,1,8,128]{3,2,1,0:T(8,128)S(1)}, f32[4,1,8,128]{3,2,1,0:T(8,128)S(1)}, u32[]{:S(2)}, u32[]{:S(2)}) collective-permute-start(f32[4,1,8,128]{3,2,1,0:T(8,128)S(1)} %get-tuple-element.165), channel_id=1, source_target_pairs={{0,16},{16,32},{32,48},{48,64},{64,80},{80,96},{96,112},{112,128},... | collective-permute-start | bytes 49160 | tf_op jit(solution)/shard_map/ppermute | solution.py:25
  7.0 18.0 %collective-permute-start.1 = (f32[4,1,8,128]{3,2,1,0:T(8,128)S(1)}, f32[4,1,8,128]{3,2,1,0:T(8,128)S(1)}, u32[]{:S(2)}, u32[]{:S(2)}) collective-permute-start(f32[4,1,8,128]{3,2,1,0:T(8,128)S(1)} %get-tuple-element.166), channel_id=1, source_target_pairs={{16,0},{32,16},{48,32},{64,48},{80,64},{96,80},{112,96},{128,112},... | collective-permute-start | bytes 49160 | tf_op jit(solution)/shard_map/ppermute | solution.py:27
  8.9 19.9 %collective-permute-start.2 = (f32[5,2,1,8,128]{4,3,2,1,0:T(8,128)S(1)}, f32[5,2,1,8,128]{4,3,2,1,0:T(8,128)S(1)}, u32[]{:S(2)}, u32[]{:S(2)}) collective-permute-start(f32[5,2,1,8,128]{4,3,2,1,0:T(8,128)S(1)} %get-tuple-element.155), channel_id=1, source_target_pairs={{0,16},{16,32},{32,48},{48,64},{64,80},{80,96},{96,112},{112,128},... | collective-permute-start | bytes 122888 | tf_op jit(solution)/shard_map/ppermute | solution.py:25
  16.2 12.7 %collective-permute-start.3 = (f32[5,2,1,8,128]{4,3,2,1,0:T(8,128)S(1)}, f32[5,2,1,8,128]{4,3,2,1,0:T(8,128)S(1)}, u32[]{:S(2)}, u32[]{:S(2)}) collective-permute-start(f32[5,2,1,8,128]{4,3,2,1,0:T(8,128)S(1)} %get-tuple-element.154), channel_id=1, source_target_pairs={{16,0},{32,16},{48,32},{64,48},{80,64},{96,80},{112,96},{128,112},... | collective-permute-start | bytes 122888 | tf_op jit(solution)/shard_map/ppermute | solution.py:27
  18.2 7.1 %collective-permute-start.4 = (f32[4,16,1,128]{3,2,1,0:T(1,128)S(1)}, f32[4,16,1,128]{3,2,1,0:T(1,128)S(1)}, u32[]{:S(2)}, u32[]{:S(2)}) collective-permute-start(f32[4,16,1,128]{3,2,1,0:T(1,128)S(1)} %get-tuple-element.167), channel_id=1, source_target_pairs={{0,1},{1,2},{2,3},{3,4},{4,5},{5,6},{6,7},{7,8},{8,9},{9,10},{10,1... | collective-permute-start | bytes 98312 | tf_op jit(solution)/shard_map/ppermute | solution.py:25
  19.6 9.1 %collective-permute-start.5 = (f32[4,16,1,128]{3,2,1,0:T(1,128)S(1)}, f32[4,16,1,128]{3,2,1,0:T(1,128)S(1)}, u32[]{:S(2)}, u32[]{:S(2)}) collective-permute-start(f32[4,16,1,128]{3,2,1,0:T(1,128)S(1)} %get-tuple-element.168), channel_id=1, source_target_pairs={{1,0},{2,1},{3,2},{4,3},{5,4},{6,5},{7,6},{8,7},{9,8},{10,9},{11,1... | collective-permute-start | bytes 98312 | tf_op jit(solution)/shard_map/ppermute | solution.py:27
  33.2 6.6 %collective-permute-start.8 = (f32[2,2,16,8]{2,3,1,0:T(8,128)S(1)}, f32[2,2,16,8]{2,3,1,0:T(8,128)S(1)}, u32[]{:S(2)}, u32[]{:S(2)}) collective-permute-start(f32[2,2,16,8]{2,3,1,0:T(8,128)S(1)} %bitcast.718), channel_id=1, source_target_pairs={{0,8},{1,9},{2,10},{3,11},{4,12},{5,13},{6,14},{7,15},{8,0},{9,1},... | collective-permute-start | bytes 6152 | tf_op jit(solution)/shard_map/ppermute | solution.py:37
  44.9 16.0 %collective-permute-start.10 = (f32[5,2,1,8,128]{4,3,2,1,0:T(8,128)S(1)}, f32[5,2,1,8,128]{4,3,2,1,0:T(8,128)S(1)}, u32[]{:S(2)}, u32[]{:S(2)}) collective-permute-start(f32[5,2,1,8,128]{4,3,2,1,0:T(8,128)S(1)} %get-tuple-element.149), channel_id=1, source_target_pairs={{16,0},{32,16},{48,32},{64,48},{80,64},{96,80},{112,96},{128,112},... | collective-permute-start | bytes 122888 | tf_op jit(solution)/shard_map/ppermute | solution.py:27
  46.8 14.1 %collective-permute-start.9 = (f32[5,2,1,8,128]{4,3,2,1,0:T(8,128)S(1)}, f32[5,2,1,8,128]{4,3,2,1,0:T(8,128)S(1)}, u32[]{:S(2)}, u32[]{:S(2)}) collective-permute-start(f32[5,2,1,8,128]{4,3,2,1,0:T(8,128)S(1)} %get-tuple-element.148), channel_id=1, source_target_pairs={{0,16},{16,32},{32,48},{48,64},{64,80},{80,96},{96,112},{112,128},... | collective-permute-start | bytes 122888 | tf_op jit(solution)/shard_map/ppermute | solution.py:25
  66.5 6.6 %collective-permute-start.13 = (f32[2,2,16,8]{2,3,1,0:T(8,128)S(1)}, f32[2,2,16,8]{2,3,1,0:T(8,128)S(1)}, u32[]{:S(2)}, u32[]{:S(2)}) collective-permute-start(f32[2,2,16,8]{2,3,1,0:T(8,128)S(1)} %bitcast.714), channel_id=1, source_target_pairs={{0,8},{1,9},{2,10},{3,11},{4,12},{5,13},{6,14},{7,15},{8,0},{9,1},... | collective-permute-start | bytes 6152 | tf_op jit(solution)/shard_map/ppermute | solution.py:37
  77.6 11.2 %collective-permute-start.14 = (f32[5,2,1,8,128]{4,3,2,1,0:T(8,128)S(1)}, f32[5,2,1,8,128]{4,3,2,1,0:T(8,128)S(1)}, u32[]{:S(2)}, u32[]{:S(2)}) collective-permute-start(f32[5,2,1,8,128]{4,3,2,1,0:T(8,128)S(1)} %get-tuple-element.142), channel_id=1, source_target_pairs={{0,16},{16,32},{32,48},{48,64},{64,80},{80,96},{96,112},{112,128},... | collective-permute-start | bytes 122888 | tf_op jit(solution)/shard_map/ppermute | solution.py:25
  83.2 8.9 %collective-permute-start.15 = (f32[5,2,1,8,128]{4,3,2,1,0:T(8,128)S(1)}, f32[5,2,1,8,128]{4,3,2,1,0:T(8,128)S(1)}, u32[]{:S(2)}, u32[]{:S(2)}) collective-permute-start(f32[5,2,1,8,128]{4,3,2,1,0:T(8,128)S(1)} %get-tuple-element.143), channel_id=1, source_target_pairs={{16,0},{32,16},{48,32},{64,48},{80,64},{96,80},{112,96},{128,112},... | collective-permute-start | bytes 122888 | tf_op jit(solution)/shard_map/ppermute | solution.py:27
  85.1 8.0 %collective-permute-start.16 = (f32[5,2,16,1,128]{4,2,3,1,0:T(8,128)S(1)}, f32[5,2,16,1,128]{4,2,3,1,0:T(8,128)S(1)}, u32[]{:S(2)}, u32[]{:S(2)}) collective-permute-start(f32[5,2,16,1,128]{4,2,3,1,0:T(8,128)S(1)} %bitcast.710), channel_id=1, source_target_pairs={{0,1},{1,2},{2,3},{3,4},{4,5},{5,6},{6,7},{7,8},{8,9},{9,10},{10,1... | collective-permute-start | bytes 245768 | tf_op jit(solution)/shard_map/ppermute | solution.py:25
  85.2 7.9 %collective-permute-start.17 = (f32[5,2,16,1,128]{4,2,3,1,0:T(8,128)S(1)}, f32[5,2,16,1,128]{4,2,3,1,0:T(8,128)S(1)}, u32[]{:S(2)}, u32[]{:S(2)}) collective-permute-start(f32[5,2,16,1,128]{4,2,3,1,0:T(8,128)S(1)} %bitcast.706), channel_id=1, source_target_pairs={{1,0},{2,1},{3,2},{4,3},{5,4},{6,5},{7,6},{8,7},{9,8},{10,9},{11,1... | collective-permute-start | bytes 245768 | tf_op jit(solution)/shard_map/ppermute | solution.py:27
  96.8 6.7 %collective-permute-start.18 = (f32[2,2,16,8]{2,3,1,0:T(8,128)S(1)}, f32[2,2,16,8]{2,3,1,0:T(8,128)S(1)}, u32[]{:S(2)}, u32[]{:S(2)}) collective-permute-start(f32[2,2,16,8]{2,3,1,0:T(8,128)S(1)} %bitcast.715), channel_id=1, source_target_pairs={{0,8},{1,9},{2,10},{3,11},{4,12},{5,13},{6,14},{7,15},{8,0},{9,1},... | collective-permute-start | bytes 6152 | tf_op jit(solution)/shard_map/ppermute | solution.py:37
  107.4 12.8 %collective-permute-start.19 = (f32[5,2,1,8,128]{4,3,2,1,0:T(8,128)S(1)}, f32[5,2,1,8,128]{4,3,2,1,0:T(8,128)S(1)}, u32[]{:S(2)}, u32[]{:S(2)}) collective-permute-start(f32[5,2,1,8,128]{4,3,2,1,0:T(8,128)S(1)} %get-tuple-element.136), channel_id=1, source_target_pairs={{0,16},{16,32},{32,48},{48,64},{64,80},{80,96},{96,112},{112,128},... | collective-permute-start | bytes 122888 | tf_op jit(solution)/shard_map/ppermute | solution.py:25
  114.6 8.9 %collective-permute-start.20 = (f32[5,2,1,8,128]{4,3,2,1,0:T(8,128)S(1)}, f32[5,2,1,8,128]{4,3,2,1,0:T(8,128)S(1)}, u32[]{:S(2)}, u32[]{:S(2)}) collective-permute-start(f32[5,2,1,8,128]{4,3,2,1,0:T(8,128)S(1)} %get-tuple-element.137), channel_id=1, source_target_pairs={{16,0},{32,16},{48,32},{64,48},{80,64},{96,80},{112,96},{128,112},... | collective-permute-start | bytes 122888 | tf_op jit(solution)/shard_map/ppermute | solution.py:27
  116.5 8.0 %collective-permute-start.21 = (f32[5,2,16,1,128]{4,2,3,1,0:T(8,128)S(1)}, f32[5,2,16,1,128]{4,2,3,1,0:T(8,128)S(1)}, u32[]{:S(2)}, u32[]{:S(2)}) collective-permute-start(f32[5,2,16,1,128]{4,2,3,1,0:T(8,128)S(1)} %bitcast.711), channel_id=1, source_target_pairs={{0,1},{1,2},{2,3},{3,4},{4,5},{5,6},{6,7},{7,8},{8,9},{9,10},{10,1... | collective-permute-start | bytes 245768 | tf_op jit(solution)/shard_map/ppermute | solution.py:25
  116.6 7.9 %collective-permute-start.22 = (f32[5,2,16,1,128]{4,2,3,1,0:T(8,128)S(1)}, f32[5,2,16,1,128]{4,2,3,1,0:T(8,128)S(1)}, u32[]{:S(2)}, u32[]{:S(2)}) collective-permute-start(f32[5,2,16,1,128]{4,2,3,1,0:T(8,128)S(1)} %bitcast.707), channel_id=1, source_target_pairs={{1,0},{2,1},{3,2},{4,3},{5,4},{6,5},{7,6},{8,7},{9,8},{10,9},{11,1... | collective-permute-start | bytes 245768 | tf_op jit(solution)/shard_map/ppermute | solution.py:27
  127.4 6.6 %collective-permute-start.23 = (f32[2,2,16,8]{2,3,1,0:T(8,128)S(1)}, f32[2,2,16,8]{2,3,1,0:T(8,128)S(1)}, u32[]{:S(2)}, u32[]{:S(2)}) collective-permute-start(f32[2,2,16,8]{2,3,1,0:T(8,128)S(1)} %bitcast.716), channel_id=1, source_target_pairs={{0,8},{1,9},{2,10},{3,11},{4,12},{5,13},{6,14},{7,15},{8,0},{9,1},... | collective-permute-start | bytes 6152 | tf_op jit(solution)/shard_map/ppermute | solution.py:37
  137.3 12.7 %collective-permute-start.24 = (f32[5,2,1,8,128]{4,3,2,1,0:T(8,128)S(1)}, f32[5,2,1,8,128]{4,3,2,1,0:T(8,128)S(1)}, u32[]{:S(2)}, u32[]{:S(2)}) collective-permute-start(f32[5,2,1,8,128]{4,3,2,1,0:T(8,128)S(1)} %get-tuple-element.130), channel_id=1, source_target_pairs={{0,16},{16,32},{32,48},{48,64},{64,80},{80,96},{96,112},{112,128},... | collective-permute-start | bytes 122888 | tf_op jit(solution)/shard_map/ppermute | solution.py:25
  144.5 8.9 %collective-permute-start.25 = (f32[5,2,1,8,128]{4,3,2,1,0:T(8,128)S(1)}, f32[5,2,1,8,128]{4,3,2,1,0:T(8,128)S(1)}, u32[]{:S(2)}, u32[]{:S(2)}) collective-permute-start(f32[5,2,1,8,128]{4,3,2,1,0:T(8,128)S(1)} %get-tuple-element.131), channel_id=1, source_target_pairs={{16,0},{32,16},{48,32},{64,48},{80,64},{96,80},{112,96},{128,112},... | collective-permute-start | bytes 122888 | tf_op jit(solution)/shard_map/ppermute | solution.py:27
  146.4 8.0 %collective-permute-start.26 = (f32[5,2,16,1,128]{4,2,3,1,0:T(8,128)S(1)}, f32[5,2,16,1,128]{4,2,3,1,0:T(8,128)S(1)}, u32[]{:S(2)}, u32[]{:S(2)}) collective-permute-start(f32[5,2,16,1,128]{4,2,3,1,0:T(8,128)S(1)} %bitcast.712), channel_id=1, source_target_pairs={{0,1},{1,2},{2,3},{3,4},{4,5},{5,6},{6,7},{7,8},{8,9},{9,10},{10,1... | collective-permute-start | bytes 245768 | tf_op jit(solution)/shard_map/ppermute | solution.py:25
  146.5 7.9 %collective-permute-start.27 = (f32[5,2,16,1,128]{4,2,3,1,0:T(8,128)S(1)}, f32[5,2,16,1,128]{4,2,3,1,0:T(8,128)S(1)}, u32[]{:S(2)}, u32[]{:S(2)}) collective-permute-start(f32[5,2,16,1,128]{4,2,3,1,0:T(8,128)S(1)} %bitcast.708), channel_id=1, source_target_pairs={{1,0},{2,1},{3,2},{4,3},{5,4},{6,5},{7,6},{8,7},{9,8},{10,9},{11,1... | collective-permute-start | bytes 245768 | tf_op jit(solution)/shard_map/ppermute | solution.py:27
  158.0 6.6 %collective-permute-start.28 = (f32[2,2,16,8]{2,3,1,0:T(8,128)S(1)}, f32[2,2,16,8]{2,3,1,0:T(8,128)S(1)}, u32[]{:S(2)}, u32[]{:S(2)}) collective-permute-start(f32[2,2,16,8]{2,3,1,0:T(8,128)S(1)} %bitcast.717), channel_id=1, source_target_pairs={{0,8},{1,9},{2,10},{3,11},{4,12},{5,13},{6,14},{7,15},{8,0},{9,1},... | collective-permute-start | bytes 6152 | tf_op jit(solution)/shard_map/ppermute | solution.py:37
  169.2 12.9 %collective-permute-start.29 = (f32[5,2,1,8,128]{4,3,2,1,0:T(8,128)S(1)}, f32[5,2,1,8,128]{4,3,2,1,0:T(8,128)S(1)}, u32[]{:S(2)}, u32[]{:S(2)}) collective-permute-start(f32[5,2,1,8,128]{4,3,2,1,0:T(8,128)S(1)} %get-tuple-element.124), channel_id=1, source_target_pairs={{0,16},{16,32},{32,48},{48,64},{64,80},{80,96},{96,112},{112,128},... | collective-permute-start | bytes 122888 | tf_op jit(solution)/shard_map/ppermute | solution.py:25
  176.5 8.9 %collective-permute-start.30 = (f32[5,2,1,8,128]{4,3,2,1,0:T(8,128)S(1)}, f32[5,2,1,8,128]{4,3,2,1,0:T(8,128)S(1)}, u32[]{:S(2)}, u32[]{:S(2)}) collective-permute-start(f32[5,2,1,8,128]{4,3,2,1,0:T(8,128)S(1)} %get-tuple-element.125), channel_id=1, source_target_pairs={{16,0},{32,16},{48,32},{64,48},{80,64},{96,80},{112,96},{128,112},... | collective-permute-start | bytes 122888 | tf_op jit(solution)/shard_map/ppermute | solution.py:27
  178.4 8.0 %collective-permute-start.31 = (f32[5,2,16,1,128]{4,2,3,1,0:T(8,128)S(1)}, f32[5,2,16,1,128]{4,2,3,1,0:T(8,128)S(1)}, u32[]{:S(2)}, u32[]{:S(2)}) collective-permute-start(f32[5,2,16,1,128]{4,2,3,1,0:T(8,128)S(1)} %bitcast.704), channel_id=1, source_target_pairs={{0,1},{1,2},{2,3},{3,4},{4,5},{5,6},{6,7},{7,8},{8,9},{9,10},{10,1... | collective-permute-start | bytes 245768 | tf_op jit(solution)/shard_map/ppermute | solution.py:25
  178.5 7.9 %collective-permute-start.32 = (f32[5,2,16,1,128]{4,2,3,1,0:T(8,128)S(1)}, f32[5,2,16,1,128]{4,2,3,1,0:T(8,128)S(1)}, u32[]{:S(2)}, u32[]{:S(2)}) collective-permute-start(f32[5,2,16,1,128]{4,2,3,1,0:T(8,128)S(1)} %bitcast.703), channel_id=1, source_target_pairs={{1,0},{2,1},{3,2},{4,3},{5,4},{6,5},{7,6},{8,7},{9,8},{10,9},{11,1... | collective-permute-start | bytes 245768 | tf_op jit(solution)/shard_map/ppermute | solution.py:27
  188.3 6.6 %collective-permute-start.33 = (f32[2,2,16,8]{2,3,1,0:T(8,128)S(1)}, f32[2,2,16,8]{2,3,1,0:T(8,128)S(1)}, u32[]{:S(2)}, u32[]{:S(2)}) collective-permute-start(f32[2,2,16,8]{2,3,1,0:T(8,128)S(1)} %bitcast.713), channel_id=1, source_target_pairs={{0,8},{1,9},{2,10},{3,11},{4,12},{5,13},{6,14},{7,15},{8,0},{9,1},... | collective-permute-start | bytes 6152 | tf_op jit(solution)/shard_map/ppermute | solution.py:37
  198.5 9.2 %collective-permute-start.34 = (f32[2,16,8,128]{3,2,1,0:T(8,128)S(1)}, f32[2,16,8,128]{3,2,1,0:T(8,128)S(1)}, u32[]{:S(2)}, u32[]{:S(2)}) collective-permute-start(f32[2,16,8,128]{3,2,1,0:T(8,128)S(1)} %slice_bitcast_fusion), channel_id=1, source_target_pairs={{0,16},{16,32},{32,48},{48,64},{64,80},{80,96},{96,112},{112,128},... | collective-permute-start | bytes 393224 | tf_op jit(solution)/shard_map/ppermute | solution.py:25
  205.7 9.9 %collective-permute-start.35 = (f32[2,16,8,128]{3,2,1,0:T(8,128)S(1)}, f32[2,16,8,128]{3,2,1,0:T(8,128)S(1)}, u32[]{:S(2)}, u32[]{:S(2)}) collective-permute-start(f32[2,16,8,128]{3,2,1,0:T(8,128)S(1)} %slice_bitcast_fusion), channel_id=1, source_target_pairs={{16,0},{32,16},{48,32},{64,48},{80,64},{96,80},{112,96},{128,112},... | collective-permute-start | bytes 393224 | tf_op jit(solution)/shard_map/ppermute | solution.py:27
  (28 other events, 110.5 us)
where the time goes:
time: 218 us; the launch traced here: 217 us
  starting transfers between devices  128 us (59%)
  other arithmetic  35.2 us (16%)
  waiting for transfers between devices  27.7 us (13%)
  local copies, waits for them, and re-layouts  23.7 us (11%)
  between operations  2.35 us (1%)
    ppermute x15, starting transfers between devices, extended(): lax.ppermute(tail, axis, [(i, (i + 1) % count) for i in range(ends)])  58.3 us
    ppermute x15, starting transfers between devices, extended(): lax.ppermute(head, axis, [((i + 1) % count, i) for i in range(ends)])  42 us
    ppermute x6, starting transfers between devices, shifted_2(): return lax.ppermute(value, axis, pairs)  27.6 us
    ppermute x15, waiting for transfers between devices, extended(): lax.ppermute(head, axis, [((i + 1) % count, i) for i in range(ends)])  21.3 us
    unnamed x50, local copies, waits for them, and re-layouts  7.21 us
    mul x6, other arithmetic, per_device(): along_r = (padded[..., 2:] - padded[..., :-2]) * (0.5 / radius)  6.71 us
    mul x5, other arithmetic, per_device(): (wrapped[:, :, :, 2:] - wrapped[:, :, :, :-2]) * (0.5 / (azimuth_step * r...  6.43 us
    slice x6, local copies, waits for them, and re-layouts, per_device(): mirrored = shifted_2(radial[..., 0], 'az', sectors // 2)  6.25 us
  transfers between devices with their start and end apart: 36, of which 14 were waited for; matrix products, arithmetic and copies ran while one was open for 6% of the time, Pallas kernels for 0%

commit v1 on v0

v1 whole, which is shorter than its diff:
```python
import functools
import math

import jax
import jax.numpy as jnp
from jax import lax
from jax.experimental import pallas as pl
from jax.experimental.pallas import tpu as pltpu
from jax.sharding import PartitionSpec as P

SEP = 16
SECTIONS = 6
NAXIAL = 2048
FREQUENCY = 0.7
MESH = pl.DeviceIdType.MESH
CHUNK = 4


def kernel(
    n_ax, n_az,
    start, adjoint, mean_flow, forcing, tke, half_width,
    green, intensity,
    state, partial, coef, force, sigma, amp, width, weights, flow, result,
    flux_x, flux_l, send_x, recv_x, recv_t, send_o, recv_o, pressure,
    load_sem, store_sem, x_send, x_recv, t_send, t_recv, o_send, o_recv, p_send, p_recv,
):
    cells, sector, radial = state.shape[3], state.shape[4], state.shape[5]
    ax, az = lax.axis_index("ax"), lax.axis_index("az")
    left, right = ax - 1, ax + 1
    below, above = lax.rem(az + n_az - 1, n_az), lax.rem(az + 1, n_az)
    opposite = lax.rem(az + n_az // 2, n_az)
    has_left, has_right = ax > 0, ax < n_ax - 1

    loads = [
        pltpu.make_async_copy(src, dst, load_sem.at[n])
        for n, (src, dst) in enumerate(
            [(mean_flow, flow), (adjoint, state.at[0]), (forcing, force), (half_width, width), (tke, amp)]
        )
    ]
    for load in loads:
        load.start()

    barrier = pltpu.get_barrier_semaphore()
    for k in (below, above, opposite):
        pl.semaphore_signal(barrier, inc=1, device_id=(ax, k), device_id_type=MESH)

    @pl.when(has_left)
    def _():
        pl.semaphore_signal(barrier, inc=1, device_id=(left, az), device_id_type=MESH)

    @pl.when(has_right)
    def _():
        pl.semaphore_signal(barrier, inc=1, device_id=(right, az), device_id_type=MESH)

    step_t = 2 * math.pi / (sector * n_az)
    lane = lax.broadcasted_iota(jnp.int32, (sector, radial), 1)
    row = lax.broadcasted_iota(jnp.int32, (sector, radial), 0)
    radius = lane.astype(jnp.float32) + 0.5
    tau = 0.8 / (2.0 + 1.0 / (radius * step_t))
    turn = 0.5 / (step_t * radius)
    outward = jnp.where(lane == radial - 1, 0.0, 0.5 * (radius + 1.0) / radius)
    inward = jnp.where(lane == 0, 0.0, 0.5 * (radius - 1.0) / radius)
    up = jnp.where(row == sector - 1, 0.0, turn)
    down = jnp.where(row == 0, 0.0, turn)
    edge = jnp.where(row == 0, -turn, turn)
    is_edge = (row == 0) | (row == sector - 1)
    is_axis = lane == 0

    first = start[0] + ax * cells
    pos = first + lax.broadcasted_iota(jnp.int32, (cells, sector, radial), 0)
    sigma[...] = 0.5 * (pos.astype(jnp.float32) + 0.5) / NAXIAL

    flux_x[:, :, 0] = jnp.zeros((5, 2, sector, radial), jnp.float32)
    flux_x[:, :, cells + 1] = jnp.zeros((5, 2, sector, radial), jnp.float32)

    @pl.when(jnp.logical_not(has_left))
    def _():
        pressure[:, 0:cells] = jnp.zeros((2, cells, sector, radial), jnp.float32)

    @pl.when(jnp.logical_not(has_right))
    def _():
        pressure[:, 2 * cells : 3 * cells] = jnp.zeros((2, cells, sector, radial), jnp.float32)

    def t_copy(s, way):
        source, target, who = ((sector - 1, 0, above), (0, sector - 1, below))[way]
        return pltpu.make_async_remote_copy(
            src_ref=flux_l.at[s, pl.ds(0, 4), :, source],
            dst_ref=recv_t.at[s, :, :, target],
            send_sem=t_send.at[s, way], recv_sem=t_recv.at[s, way],
            device_id=(ax, who), device_id_type=MESH,
        )

    def x_copy(s, way):
        return pltpu.make_async_remote_copy(
            src_ref=send_x.at[s, way], dst_ref=recv_x.at[s, way],
            send_sem=x_send.at[s, way], recv_sem=x_recv.at[s, way],
            device_id=((right, left)[way], az), device_id_type=MESH,
        )

    def o_copy(s):
        return pltpu.make_async_remote_copy(
            src_ref=send_o.at[s], dst_ref=recv_o.at[s],
            send_sem=o_send.at[s], recv_sem=o_recv.at[s],
            device_id=(ax, opposite), device_id_type=MESH,
        )

    def p_copy(way):
        return pltpu.make_async_remote_copy(
            src_ref=pressure.at[:, pl.ds(cells, cells)],
            dst_ref=pressure.at[:, pl.ds((0, 2 * cells)[way], cells)],
            send_sem=p_send.at[way], recv_sem=p_recv.at[way],
            device_id=((right, left)[way], az), device_id_type=MESH,
        )

    def fluxes(s, i, q, gathered):
        at = pl.ds(i, CHUNK)
        u, rho, stiff, inv = coef[0, at], coef[1, at], coef[2, at], coef[3, at]
        a, b, c, d, e = q
        shared = rho * a + stiff * e
        turned, spread = d * inv, c * inv
        along = (u * a, shared + u * b, u * c, u * d, b * inv + u * e)
        for n, f in enumerate(along):
            flux_x[n, :, pl.ds(i + 1, CHUNK)] = f
            if i == 0:
                send_x[s, 1, n] = f[:, 0]
            if i == cells - CHUNK:
                send_x[s, 0, n] = f[:, CHUNK - 1]
        flux_l[s, 0:2, at] = shared
        flux_l[s, 2:4, at] = turned
        flux_l[s, 4:6, at] = spread
        for part in range(2):
            for n, f in ((part, shared), (part + 2, spread)):
                for k in range(CHUNK):
                    to = n * cells + i + k
                    value = f[part, k] if to == 0 else pltpu.roll(f[part, k], to, 1)
                    gathered = jnp.where(lane == to, value, gathered)
        return gathered

    def send(s):
        o_copy(s).start()
        t_copy(s, 0).start()
        t_copy(s, 1).start()

        @pl.when(has_right)
        def _():
            x_copy(s, 0).start()

        @pl.when(has_left)
        def _():
            x_copy(s, 1).start()

    def weight_of(s):
        third = lax.rem(s, 3)
        return jnp.where(third == 0, 1.0 / 3.0, jnp.where(third == 1, 0.5, 1.0))

    def inner(s):
        source = lax.rem(s, 3)
        scale = weight_of(s) * tau

        def body(t, carry):
            i = t * CHUNK
            at = pl.ds(i, CHUNK)
            damp = sigma[at]
            shared, turned, spread = flux_l[s, 0:2, at], flux_l[s, 2:4, at], flux_l[s, 4:6, at]

            def radially(f):
                return outward * pltpu.roll(f, radial - 1, 3) - inward * pltpu.roll(f, 1, 3)

            def around(f):
                return up * pltpu.roll(f, sector - 1, 2) - down * pltpu.roll(f, 1, 2)

            extra = (None, None, radially(shared), around(shared), radially(spread) + around(turned) + force[:, at])
            for n in range(5):
                q = state[source, n, :, at]
                total = 0.5 * (flux_x[n, :, pl.ds(i + 2, CHUNK)] - flux_x[n, :, at]) - damp * q
                if extra[n] is not None:
                    total = total + extra[n]
                base = state[0, n, :, at]
                partial[n, 0, at] = base[0] + scale * (total[0] + FREQUENCY * q[1])
                partial[n, 1, at] = base[1] + scale * (total[1] - FREQUENCY * q[0])
            return carry

        lax.fori_loop(0, cells // CHUNK, body, 0)

    def receive(s):
        half = 0.5 * weight_of(s) * tau

        @pl.when(has_left)
        def _():
            x_copy(s, 0).wait_recv()
            partial[:, :, 0] = partial[:, :, 0] - half * recv_x[s, 0]

        @pl.when(has_right)
        def _():
            x_copy(s, 1).wait_recv()
            partial[:, :, cells - 1] = partial[:, :, cells - 1] + half * recv_x[s, 1]

        t_copy(s, 0).wait_recv()
        t_copy(s, 1).wait_recv()
        o_copy(s).wait_recv()

    def outer(s, finish):
        scale = weight_of(s) * tau
        rows = scale * edge
        mirrored = (-0.5 * scale) * 1.0
        mirror = recv_o[s]
        target = lax.rem(s + 1, 3)
        gathered = jnp.zeros((sector, radial), jnp.float32)
        for i in range(0, cells, CHUNK):
            at = pl.ds(i, CHUNK)
            q = [partial[n, :, at] for n in range(5)]
            ring = jnp.where(is_edge, recv_t[s, :, at], 0.0) * rows
            spun = [
                jnp.stack(
                    [
                        jnp.stack(
                            [
                                jnp.where(
                                    is_axis,
                                    mirrored * pltpu.roll(mirror, (radial - n * cells - i - k) % radial, 1),
                                    0.0,
                                )
                                for k in range(CHUNK)
                            ]
                        )
                        for n in (c, c + 1)
                    ]
                )
                for c in (0, 2)
            ]
            q[2] = q[2] + spun[0]
            q[3] = q[3] + ring[0:2]
            q[4] = q[4] + ring[2:4] + spun[1]
            for n in range(5):
                state[target, n, :, at] = q[n]
            if finish:
                pressure[:, pl.ds(cells + i, CHUNK)] = q[4]
            else:
                gathered = fluxes(s + 1, i, q, gathered)
        if not finish:
            send_o[s + 1] = gathered

    loads[0].wait()
    rho = flow[1]
    coef[0] = flow[0]
    coef[1] = rho
    coef[2] = rho * flow[2]
    coef[3] = 1.0 / rho
    loads[1].wait()
    gathered = jnp.zeros((sector, radial), jnp.float32)
    for i in range(0, cells, CHUNK):
        gathered = fluxes(0, i, [state[0, n, :, pl.ds(i, CHUNK)] for n in range(5)], gathered)
    send_o[0] = gathered

    pl.semaphore_wait(barrier, 3 + has_left.astype(jnp.int32) + has_right.astype(jnp.int32))
    send(0)

    loads[2].wait()
    loads[3].wait()
    loads[4].wait()

    def weigh(i, carry):
        length = width[i].astype(jnp.float32)
        inverse = 1.0 / (length * length)
        for shift in range(1, SEP + 1):
            weights[shift - 1, i] = jnp.exp(-(shift * shift) * inverse)
        return carry

    lax.fori_loop(0, cells, weigh, 0)

    def section(s, carry):
        inner(s)
        receive(s)
        outer(s, False)
        send(s + 1)
        return carry

    lax.fori_loop(0, SECTIONS - 1, section, 0)
    last = SECTIONS - 1
    inner(last)
    receive(last)
    outer(last, True)

    @pl.when(has_right)
    def _():
        p_copy(0).start()

    @pl.when(has_left)
    def _():
        p_copy(1).start()

    store = pltpu.make_async_copy(state.at[0], green, store_sem.at[0])
    store.start()

    @pl.when(has_left)
    def _():
        p_copy(0).wait_recv()

    @pl.when(has_right)
    def _():
        p_copy(1).wait_recv()

    def integrate(i, carry):
        re, im = pressure[0, cells + i], pressure[1, cells + i]
        sum_re, sum_im = re, im
        for shift in range(1, SEP + 1):
            w = weights[shift - 1, i]
            sum_re = sum_re + w * (pressure[0, cells + i + shift] + pressure[0, cells + i - shift])
            sum_im = sum_im + w * (pressure[1, cells + i + shift] + pressure[1, cells + i - shift])
        result[i] = amp[i] * (re * sum_re + im * sum_im)
        return carry

    lax.fori_loop(0, cells, integrate, 0)
    store_2 = pltpu.make_async_copy(result, intensity, store_sem.at[1])
    store_2.start()

    def drain(s, carry):
        o_copy(s).wait_send()
        t_copy(s, 0).wait_send()
        t_copy(s, 1).wait_send()

        @pl.when(has_right)
        def _():
            x_copy(s, 0).wait_send()

        @pl.when(has_left)
        def _():
            x_copy(s, 1).wait_send()

        return carry

    lax.fori_loop(0, SECTIONS, drain, 0)

    @pl.when(has_right)
    def _():
        p_copy(0).wait_send()

    @pl.when(has_left)
    def _():
        p_copy(1).wait_send()

    store.wait()
    store_2.wait()


def per_device(n_ax, n_az, adjoint, mean_flow, forcing, tke, half_width, start):
    cells, sector, radial = tke.shape
    block = (cells, sector, radial)
    f32 = jnp.float32
    any_spec = pl.BlockSpec(memory_space=pl.ANY)
    dma = pltpu.SemaphoreType.DMA
    vmem = lambda *shape: pltpu.VMEM(shape, f32)
    return pl.pallas_call(
        functools.partial(kernel, n_ax, n_az),
        out_shape=(
            jax.ShapeDtypeStruct(adjoint.shape, f32),
            jax.ShapeDtypeStruct(tke.shape, f32),
        ),
        in_specs=[pl.BlockSpec(memory_space=pltpu.SMEM)] + [any_spec] * 5,
        out_specs=(any_spec, any_spec),
        scratch_shapes=[
            vmem(3, 5, 2, *block),
            vmem(5, 2, *block),
            vmem(4, *block),
            vmem(2, *block),
            vmem(*block),
            vmem(*block),
            pltpu.VMEM(block, jnp.int32),
            vmem(SEP, *block),
            vmem(3, *block),
            vmem(*block),
            vmem(5, 2, cells + 2, sector, radial),
            vmem(SECTIONS, 6, *block),
            vmem(SECTIONS, 2, 5, 2, sector, radial),
            vmem(SECTIONS, 2, 5, 2, sector, radial),
            vmem(SECTIONS, 4, *block),
            vmem(SECTIONS, sector, radial),
            vmem(SECTIONS, sector, radial),
            vmem(2, 3 * cells, sector, radial),
            dma((5,)), dma((2,)),
            dma((SECTIONS, 2)), dma((SECTIONS, 2)),
            dma((SECTIONS, 2)), dma((SECTIONS, 2)),
            dma((SECTIONS,)), dma((SECTIONS,)),
            dma((2,)), dma((2,)),
        ],
        compiler_params=pltpu.CompilerParams(
            collective_id=0, has_side_effects=True, vmem_limit_bytes=60 * 2**20
        ),
    )(start, adjoint, mean_flow, forcing, tke, half_width)


def solution(mesh):
    return jax.shard_map(
        functools.partial(per_device, mesh.shape["ax"], mesh.shape["az"]),
        mesh=mesh,
        in_specs=(
            P(None, None, "ax", "az", None),
            P(None, "ax", "az", None),
            P(None, "ax", "az", None),
            P("ax", "az", None),
            P("ax", "az", None),
            P(),
        ),
        out_specs=(P(None, None, "ax", "az", None), P("ax", "az", None)),
        check_vma=False,
    )
```

time: 218 us -> 47.7 us (0.22)
  starting transfers between devices: 128 us -> 0 us
  Pallas kernels: 0 us -> 43.6 us
  other arithmetic: 35.2 us -> 0 us
  waiting for transfers between devices: 27.7 us -> 0 us
  local copies, waits for them, and re-layouts: 23.7 us -> 2.64 us
    ppermute x36 -> x0, starting transfers between devices: 128 us -> none  [the longest x15 58.3 us: extended(): lax.ppermute(tail, axis, [(i, (i + 1) % count) for i in range(ends)])]
    pallas_call x0 -> x1, Pallas kernels: none -> 43.6 us  [per_device(): pl.pallas_call(functools.partial(kernel, n_ax, n_az), out_shape=(jax.Shap...]
    ppermute x36 -> x0, waiting for transfers between devices: 27.7 us -> none  [the longest x15 21.3 us: extended(): lax.ppermute(head, axis, [((i + 1) % count, i) for i in range(ends)])]
    mul x38 -> x0, other arithmetic: 20.1 us -> none  [the longest x6 6.71 us: per_device(): along_r = (padded[..., 2:] - padded[..., :-2]) * (0.5 / radius)]
    slice x27 -> x0, local copies, waits for them, and re-layouts: 11.3 us -> none  [the longest x6 6.25 us: per_device(): mirrored = shifted_2(radial[..., 0], 'az', sectors // 2)]
    add x25 -> x0, other arithmetic: 6.68 us -> none  [the longest x6 4.81 us: shared_flux(): return coeffs[1][None] * state[0] + coeffs[2][None] * state[4]]
    mul x7 -> x0, local copies, waits for them, and re-layouts: 5.2 us -> none  [the longest x6 5.18 us: per_device(): 0.5 * mirrored[..., None]]
    unnamed x50 -> x4, local copies, waits for them, and re-layouts: 7.21 us -> 2.64 us
  transfers between devices with their start and end apart: 36 -> 0, of which waited for: 14 -> 0; matrix products, arithmetic and copies ran while one was open for 6% -> 0% of each run, Pallas kernels for 0% -> 0%
where the time goes in v1:
time: 47.7 us; the launch traced here: 47.6 us
  Pallas kernels  43.6 us (91%)
  local copies, waits for them, and re-layouts  2.64 us (6%)
  between operations  1.3 us (3%)
    pallas_call x1, Pallas kernels, per_device(): pl.pallas_call(functools.partial(kernel, n_ax, n_az), out_shape=(jax.Shap...  43.6 us
    unnamed x4, local copies, waits for them, and re-layouts  2.64 us

profile of v1, /device:TPU:7, one launch (start us, length us, event | category | flops | bytes accessed | tf_op | source)
XLA Modules:
  0.0 47.6 jit_solution(16871972587120842948)
XLA Ops:
  1.3 43.6 %shard_map.77 = (f32[5,2,16,8,128]{4,3,2,1,0:T(8,128)}, f32[16,8,128]{2,1,0:T(8,128)}) custom-call(s32[1]{0:T(128)S(6)} %copy.10.start, f32[5,2,16,8,128]{4,3,2,1,0:T(8,128)} %adjoint.1, f32[3,16,8,128]{3,2,1,0:T(8,128)} %mean_flow.1, f32[2,16,8,128]{3,2,1,0:T(8,128)} %forcing.1, f32[16,8,128]{2,1,0:T(8,128)} %tke.1, s32[16,8,128]{2,1,0:T(8,128)} %half_width.1), custom_call_target="tpu_custom_call" | custom-call | tf_op jit(solution)/shard_map/pallas_call | solution.py:353
  44.9 0.0 copy-start
  44.9 2.0 %copy.11 = f32[5,2,16,8,128]{4,3,2,1,0:T(8,128)} copy(f32[5,2,16,8,128]{4,3,2,1,0:T(8,128)} %get-tuple-element.4) | data formatting | bytes 1310720
  46.9 0.0 copy-done
  46.9 0.6 %copy.12 = f32[16,8,128]{2,1,0:T(8,128)} copy(f32[16,8,128]{2,1,0:T(8,128)S(1)} %copy-done) | data formatting | bytes 131072
Async XLA Ops:
  44.9 2.0 %copy-start = (f32[16,8,128]{2,1,0:T(8,128)S(1)}, f32[16,8,128]{2,1,0:T(8,128)}, u32[]{:S(2)}) copy-start(f32[16,8,128]{2,1,0:T(8,128)} %get-tuple-element.5) | copy-start | bytes 196612

commit v2 on v1

v2 whole, which is shorter than its diff:
```python
import functools
import math

import jax
import jax.numpy as jnp
from jax import lax
from jax.experimental import pallas as pl
from jax.experimental.pallas import tpu as pltpu
from jax.sharding import PartitionSpec as P

SEP = 16
SECTIONS = 6
ROUNDS = 3
NAXIAL = 2048
FREQUENCY = 0.7
MESH = pl.DeviceIdType.MESH
CHUNK = 4


def lane_pack(lane, gathered, value, to):
    moved = value if to == 0 else pltpu.roll(value, to, 1)
    return jnp.where(lane == to, moved, gathered)


def kernel(
    n_ax, n_az,
    start, adjoint, mean_flow, forcing, tke, half_width,
    green, intensity,
    state, partial, coef, force, sigma, amp, width, weights, flow, result,
    flux_x, flux_l, part_l, send_x, recv_x, recv_t, send_o, recv_o,
    send_d, recv_d, recv_a, send_p, recv_p, coef_x, coef_t, send_c, coef_o, pressure,
    load_sem, store_sem, x_send, x_recv, t_send, t_recv, o_send, o_recv, p_send, p_recv,
    d_send, d_recv, a_send, a_recv, b_send, b_recv, cx_send, cx_recv, ct_send, ct_recv, co_send, co_recv,
):
    cells, sector, radial = state.shape[3], state.shape[4], state.shape[5]
    ax, az = lax.axis_index("ax"), lax.axis_index("az")
    half_turn = n_az // 2
    left, right = ax - 1, ax + 1
    below, above = lax.rem(az + n_az - 1, n_az), lax.rem(az + 1, n_az)
    opposite = lax.rem(az + half_turn, n_az)
    opposite_below, opposite_above = lax.rem(az + half_turn - 1, n_az), lax.rem(az + half_turn + 1, n_az)
    has_left, has_right = ax > 0, ax < n_ax - 1
    sides = ((right, has_right), (left, has_left))
    turns = ((above, sector - 1, 0), (below, 0, sector - 1))

    loads = [
        pltpu.make_async_copy(src, dst, load_sem.at[n])
        for n, (src, dst) in enumerate(
            [(mean_flow, flow), (adjoint, state.at[0]), (forcing, force), (half_width, width), (tke, amp)]
        )
    ]
    for load in loads:
        load.start()

    barrier = pltpu.get_barrier_semaphore()

    def greet(i, k):
        pl.semaphore_signal(barrier, inc=1, device_id=(i, k), device_id_type=MESH)

    for i, there in sides:
        @pl.when(there)
        def _():
            for k in (opposite, below, above, az):
                greet(i, k)

    for k in (opposite_below, opposite_above, opposite, below, above):
        greet(ax, k)

    step_t = 2 * math.pi / (sector * n_az)
    lane = lax.broadcasted_iota(jnp.int32, (sector, radial), 1)
    row = lax.broadcasted_iota(jnp.int32, (sector, radial), 0)
    radius = lane.astype(jnp.float32) + 0.5
    tau = 0.8 / (2.0 + 1.0 / (radius * step_t))
    turn = 0.5 / (step_t * radius)
    outward = jnp.where(lane == radial - 1, 0.0, 0.5 * (radius + 1.0) / radius)
    inward = jnp.where(lane == 0, 0.0, 0.5 * (radius - 1.0) / radius)
    up = jnp.where(row == sector - 1, 0.0, turn)
    down = jnp.where(row == 0, 0.0, turn)
    is_edge = (row == 0) | (row == sector - 1)
    is_axis = lane == 0
    edge = jnp.where(row == 0, -turn, jnp.where(row == sector - 1, turn, 0.0))
    tau_0 = 0.8 / (2.0 + 1.0 / (0.5 * step_t))
    turn_0 = 0.5 / (step_t * 0.5)
    edge_0 = jnp.where(row == 0, -turn_0, jnp.where(row == sector - 1, turn_0, 0.0))

    first = start[0] + ax * cells
    pos = first + lax.broadcasted_iota(jnp.int32, (cells, sector, radial), 0)
    sigma[...] = 0.5 * (pos.astype(jnp.float32) + 0.5) / NAXIAL

    flux_x[:, :, 0] = jnp.zeros((5, 2, sector, radial), jnp.float32)
    flux_x[:, :, cells + 1] = jnp.zeros((5, 2, sector, radial), jnp.float32)

    @pl.when(jnp.logical_not(has_left))
    def _():
        pressure[:, 0:cells] = jnp.zeros((2, cells, sector, radial), jnp.float32)

    @pl.when(jnp.logical_not(has_right))
    def _():
        pressure[:, 2 * cells : 3 * cells] = jnp.zeros((2, cells, sector, radial), jnp.float32)

    def remote(src, dst, send_sem, recv_sem, i, k):
        return pltpu.make_async_remote_copy(
            src_ref=src, dst_ref=dst, send_sem=send_sem, recv_sem=recv_sem,
            device_id=(i, k), device_id_type=MESH,
        )

    def t_copy(r, later, way):
        who, mine, its = turns[way]
        source = part_l.at[r] if later else flux_l.at[2 * r, pl.ds(0, 4)]
        s = 2 * r + later
        return remote(
            source.at[:, :, mine], recv_t.at[s, :, :, its], t_send.at[s, way], t_recv.at[s, way], ax, who
        )

    def x_copy(s, way):
        return remote(send_x.at[s, way], recv_x.at[s, way], x_send.at[s, way], x_recv.at[s, way], sides[way][0], az)

    def o_copy(s):
        return remote(send_o.at[s], recv_o.at[s], o_send.at[s], o_recv.at[s], ax, opposite)

    def d_copy(r, way, spin):
        who, mine, its = turns[spin]
        return remote(
            send_d.at[r, way, :, mine], recv_d.at[r, way, :, its],
            d_send.at[r, way, spin], d_recv.at[r, way, spin], sides[way][0], who,
        )

    def a_copy(r, spin):
        _, mine, its = turns[spin]
        return remote(
            send_o.at[2 * r, pl.ds(mine, 1)], recv_a.at[r, pl.ds(its, 1)], a_send.at[r, spin], a_recv.at[r, spin],
            ax, (opposite_above, opposite_below)[spin],
        )

    def b_copy(r, way):
        return remote(
            send_p.at[r, way], recv_p.at[r, way], b_send.at[r, way], b_recv.at[r, way], sides[way][0], opposite
        )

    def cx_copy(way):
        return remote(
            coef.at[:, (cells - 1, 0)[way]], coef_x.at[way], cx_send.at[way], cx_recv.at[way], sides[way][0], az
        )

    def ct_copy(way):
        who, mine, its = turns[way]
        return remote(
            coef.at[pl.ds(1, 3), :, mine], coef_t.at[:, :, its], ct_send.at[way], ct_recv.at[way], ax, who
        )

    def co_copy():
        return remote(send_c, coef_o, co_send.at[0], co_recv.at[0], ax, opposite)

    def p_copy(way):
        return remote(
            pressure.at[:, pl.ds(cells, cells)], pressure.at[:, pl.ds((0, 2 * cells)[way], cells)],
            p_send.at[way], p_recv.at[way], sides[way][0], az,
        )

    def axial(q, u, rho, stiff, inv):
        a, b, c, d, e = q
        return (u * a, rho * a + stiff * e + u * b, u * c, u * d, b * inv + u * e)

    def fluxes(s, i, q, gathered):
        at = pl.ds(i, CHUNK)
        u, rho, stiff, inv = coef[0, at], coef[1, at], coef[2, at], coef[3, at]
        a, b, c, d, e = q
        shared = rho * a + stiff * e
        turned, spread = d * inv, c * inv
        along = (u * a, shared + u * b, u * c, u * d, b * inv + u * e)
        for n, f in enumerate(along):
            flux_x[n, :, pl.ds(i + 1, CHUNK)] = f
        flux_l[s, 0:2, at] = shared
        flux_l[s, 2:4, at] = turned
        flux_l[s, 4:6, at] = spread
        if gathered is None:
            return None
        r = s // 2
        for way, end, k in ((1, 0, 0), (0, cells - CHUNK, CHUNK - 1)):
            if i == end:
                for n, f in enumerate(along):
                    send_x[s, way, n] = f[:, k]
                for n, f in enumerate((along[0], along[3], along[4], shared, turned)):
                    send_d[r, way, 2 * n : 2 * n + 2] = f[:, k]
                packed = jnp.zeros((sector, radial), jnp.float32)
                for n, f in enumerate((shared, spread, along[0], along[2], along[4])):
                    for part in range(2):
                        packed = lane_pack(lane, packed, f[part, k], 2 * n + part)
                send_p[r, way] = packed
        for n, f in enumerate((shared, spread, turned)):
            for part in range(2):
                for k in range(CHUNK):
                    gathered[n] = lane_pack(lane, gathered[n], f[part, k], (2 * n + part) * cells + i + k)
        return gathered

    def nothing(count):
        return [jnp.zeros((sector, radial), jnp.float32) for _ in range(count)]

    def known(r):
        s = 2 * r + 1
        gathered = nothing(2)
        for i in range(0, cells, CHUNK):
            at = pl.ds(i, CHUNK)
            rho, stiff, inv = coef[1, at], coef[2, at], coef[3, at]
            shared = rho * partial[0, :, at] + stiff * partial[4, :, at]
            spread = partial[2, :, at] * inv
            part_l[r, 0:2, at] = shared
            part_l[r, 2:4, at] = partial[3, :, at] * inv
            for n, f in enumerate((shared, spread)):
                for part in range(2):
                    for k in range(CHUNK):
                        gathered[n] = lane_pack(lane, gathered[n], f[part, k], (2 * n + part) * cells + i + k)
        send_o[s] = jnp.where(lane < 2 * cells, gathered[0], gathered[1])
        o_copy(s).start()
        t_copy(r, 1, 0).start()
        t_copy(r, 1, 1).start()
        for way, i in ((1, 0), (0, cells - 1)):
            q = [partial[n, :, i] for n in range(5)]
            for n, f in enumerate(axial(q, coef[0, i], coef[1, i], coef[2, i], coef[3, i])):
                send_x[s, way, n] = f
        for way in range(2):
            @pl.when(sides[way][1])
            def _():
                x_copy(s, way).start()

    def send(r):
        for way in range(2):
            @pl.when(sides[way][1])
            def _():
                b_copy(r, way).start()

        a_copy(r, 0).start()
        a_copy(r, 1).start()
        o_copy(2 * r).start()
        for way in range(2):
            @pl.when(sides[way][1])
            def _():
                d_copy(r, way, 0).start()
                d_copy(r, way, 1).start()

        t_copy(r, 0, 0).start()
        t_copy(r, 0, 1).start()
        for way in range(2):
            @pl.when(sides[way][1])
            def _():
                x_copy(2 * r, way).start()

    def weight_of(s):
        third = lax.rem(s, 3)
        return jnp.where(third == 0, 1.0 / 3.0, jnp.where(third == 1, 0.5, 1.0))

    def inner(s):
        source = lax.rem(s, 3)
        scale = weight_of(s) * tau

        def body(t, carry):
            i = t * CHUNK
            at = pl.ds(i, CHUNK)
            damp = sigma[at]
            shared, turned, spread = flux_l[s, 0:2, at], flux_l[s, 2:4, at], flux_l[s, 4:6, at]

            def radially(f):
                return outward * pltpu.roll(f, radial - 1, 3) - inward * pltpu.roll(f, 1, 3)

            def around(f):
                return up * pltpu.roll(f, sector - 1, 2) - down * pltpu.roll(f, 1, 2)

            extra = (None, None, radially(shared), around(shared), radially(spread) + around(turned) + force[:, at])
            for n in range(5):
                q = state[source, n, :, at]
                total = 0.5 * (flux_x[n, :, pl.ds(i + 2, CHUNK)] - flux_x[n, :, at]) - damp * q
                if extra[n] is not None:
                    total = total + extra[n]
                base = state[0, n, :, at]
                partial[n, 0, at] = base[0] + scale * (total[0] + FREQUENCY * q[1])
                partial[n, 1, at] = base[1] + scale * (total[1] - FREQUENCY * q[0])
            return carry

        lax.fori_loop(0, cells // CHUNK, body, 0)

    def receive(r, later):
        s = 2 * r + later
        for way in range(2):
            @pl.when(sides[1 - way][1])
            def _():
                x_copy(s, way).wait_recv()

        t_copy(r, later, 0).wait_recv()
        t_copy(r, later, 1).wait_recv()
        o_copy(s).wait_recv()

    def complete(r):
        s = 2 * r + 1
        scale = weight_of(2 * r) * tau
        half = 0.5 * scale
        scale_0 = weight_of(2 * r) * tau_0
        half_0 = 0.5 * scale_0
        around = scale * edge
        a_copy(r, 0).wait_recv()
        a_copy(r, 1).wait_recv()
        aside = jnp.where(is_edge, recv_a[r], 0.0)
        axis = -half_0 * aside

        for i in range(0, cells, CHUNK):
            at = pl.ds(i, CHUNK)
            spun = jnp.stack(
                [
                    jnp.stack(
                        [
                            jnp.where(is_axis, pltpu.roll(axis, radial - (2 + part) * cells - i - k, 1), 0.0)
                            for k in range(CHUNK)
                        ]
                    )
                    for part in range(2)
                ]
            )
            more_d = -around * flux_l[2 * r, 0:2, at]
            more_e = spun - around * flux_l[2 * r, 2:4, at]
            recv_t[s, 0:2, at] = recv_t[s, 0:2, at] + coef_t[1, at] * more_e
            recv_t[s, 2:4, at] = recv_t[s, 2:4, at] + coef_t[2, at] * more_d

        mine = send_o[2 * r]
        more_c = -half_0 * pltpu.roll(mine, 2 * cells, 1)
        more_e = -half_0 * pltpu.roll(mine, radial - 2 * cells, 1) + scale_0 * edge_0 * pltpu.roll(
            aside, radial - 4 * cells, 1
        )
        recv_o[s] = (
            recv_o[s]
            + coef_o[0] * jnp.where(lane < 2 * cells, 0.0, more_c)
            + coef_o[1] * jnp.where(lane < 2 * cells, more_e, 0.0)
        )

        for way, i, sign in ((0, 0, 1.0), (1, cells - 1, -1.0)):
            @pl.when(sides[1 - way][1])
            def _():
                d_copy(r, way, 0).wait_recv()
                d_copy(r, way, 1).wait_recv()
                corner = jnp.where(is_edge, recv_d[r, way], 0.0)
                gone = (-sign * half) * corner[0:6]
                recv_t[s, 0:2, i] = recv_t[s, 0:2, i] + coef_t[0, i] * gone[0:2] + coef_t[1, i] * gone[4:6]
                recv_t[s, 2:4, i] = recv_t[s, 2:4, i] + coef_t[2, i] * gone[2:4]
                b_copy(r, way).wait_recv()
                packed = recv_p[r, way]

                def at_axis(n):
                    return jnp.stack(
                        [
                            jnp.where(is_axis, packed if n + part == 0 else pltpu.roll(packed, radial - n - part, 1), 0.0)
                            for part in range(2)
                        ]
                    )

                more = [(sign * half) * send_x[2 * r, 1 - way, n] for n in range(5)]
                more[2] = more[2] - half * at_axis(0)
                more[3] = more[3] + around * corner[6:8]
                more[4] = more[4] + around * corner[8:10] - half * at_axis(2)
                c = coef_x[way]
                for n, f in enumerate(axial(more, c[0], c[1], c[2], c[3])):
                    recv_x[s, way, n] = recv_x[s, way, n] + f

                def spread_out(n, to):
                    low = pltpu.roll(packed, (radial + to + i - n) % radial, 1)
                    high = pltpu.roll(packed, (radial + to + cells + i - n - 1) % radial, 1)
                    return jnp.where(lane == to + i, low, jnp.where(lane == to + cells + i, high, 0.0))

                recv_o[s] = recv_o[s] - (sign * half_0) * (
                    coef_o[0] * (spread_out(4, 0) + spread_out(6, 2 * cells)) + coef_o[1] * spread_out(8, 0)
                )

    def outer(s, then):
        scale = weight_of(s) * tau
        half = 0.5 * scale
        for way, i, sign in ((0, 0, -1.0), (1, cells - 1, 1.0)):
            @pl.when(sides[1 - way][1])
            def _():
                partial[:, :, i] = partial[:, :, i] + (sign * half) * recv_x[s, way]

        rows = scale * edge
        mirror = (-0.5 * tau_0) * weight_of(s) * recv_o[s]
        target = lax.rem(s + 1, 3)
        gathered = nothing(3) if then == "round" else None
        for i in range(0, cells, CHUNK):
            at = pl.ds(i, CHUNK)
            q = [partial[n, :, at] for n in range(5)]
            ring = jnp.where(is_edge, recv_t[s, :, at], 0.0) * rows
            spun = [
                jnp.stack(
                    [
                        jnp.stack(
                            [
                                jnp.where(is_axis, pltpu.roll(mirror, (radial - n * cells - i - k) % radial, 1), 0.0)
                                for k in range(CHUNK)
                            ]
                        )
                        for n in (c, c + 1)
                    ]
                )
                for c in (0, 2)
            ]
            q[2] = q[2] + spun[0]
            q[3] = q[3] + ring[0:2]
            q[4] = q[4] + ring[2:4] + spun[1]
            for n in range(5):
                state[target, n, :, at] = q[n]
            if then == "none":
                pressure[:, pl.ds(cells + i, CHUNK)] = q[4]
            else:
                gathered = fluxes(s + 1, i, q, gathered)
        if then == "round":
            join(s + 1, gathered)

    def join(s, gathered):
        send_o[s] = jnp.where(lane < 2 * cells, gathered[0], jnp.where(lane < 4 * cells, gathered[1], gathered[2]))

    loads[0].wait()
    rho = flow[1]
    coef[0] = flow[0]
    coef[1] = rho
    coef[2] = rho * flow[2]
    coef[3] = 1.0 / rho
    loads[1].wait()
    gathered = nothing(3)
    for i in range(0, cells, CHUNK):
        gathered = fluxes(0, i, [state[0, n, :, pl.ds(i, CHUNK)] for n in range(5)], gathered)
    join(0, gathered)

    there = has_left.astype(jnp.int32) + has_right.astype(jnp.int32)
    pl.semaphore_wait(barrier, 5 + 4 * there)
    send(0)

    gathered = nothing(3)
    for n, which in enumerate((1, 3, 2)):
        for i in range(cells):
            gathered[n] = lane_pack(lane, gathered[n], coef[which, i], (0, 2, 0)[n] * cells + i)
    wide = [jnp.where(lane % (2 * cells) < cells, g, pltpu.roll(g, cells, 1)) for g in gathered]
    send_c[0] = jnp.where(lane < 2 * cells, wide[0], jnp.where(lane < 4 * cells, wide[1], 0.0))
    send_c[1] = jnp.where(lane < 2 * cells, wide[2], 0.0)
    co_copy().start()
    ct_copy(0).start()
    ct_copy(1).start()
    for way in range(2):
        @pl.when(sides[way][1])
        def _():
            cx_copy(way).start()

    loads[2].wait()

    def first_half(r):
        inner(2 * r)
        known(r)
        receive(r, 0)
        outer(2 * r, "plain")
        inner(2 * r + 1)
        receive(r, 1)

    def round_(r, carry):
        first_half(r)

        @pl.when(r == 0)
        def _():
            co_copy().wait_recv()
            ct_copy(0).wait_recv()
            ct_copy(1).wait_recv()
            for way in range(2):
                @pl.when(sides[1 - way][1])
                def _():
                    cx_copy(way).wait_recv()

        complete(r)
        outer(2 * r + 1, "round")
        send(r + 1)

        @pl.when(r == 0)
        def _():
            loads[3].wait()

            def weigh(i, carry):
                length = width[i].astype(jnp.float32)
                inverse = 1.0 / (length * length)
                for shift in range(1, SEP + 1):
                    weights[shift - 1, i] = jnp.exp(-(shift * shift) * inverse)
                return carry

            lax.fori_loop(0, cells, weigh, 0)

        return carry

    lax.fori_loop(0, ROUNDS - 1, round_, 0)
    last = ROUNDS - 1
    first_half(last)
    complete(last)
    outer(2 * last + 1, "none")

    for way in range(2):
        @pl.when(sides[way][1])
        def _():
            p_copy(way).start()

    store = pltpu.make_async_copy(state.at[0], green, store_sem.at[0])
    store.start()
    loads[4].wait()
    for way in range(2):
        @pl.when(sides[1 - way][1])
        def _():
            p_copy(way).wait_recv()

    def integrate(i, carry):
        re, im = pressure[0, cells + i], pressure[1, cells + i]
        sum_re, sum_im = re, im
        for shift in range(1, SEP + 1):
            w = weights[shift - 1, i]
            sum_re = sum_re + w * (pressure[0, cells + i + shift] + pressure[0, cells + i - shift])
            sum_im = sum_im + w * (pressure[1, cells + i + shift] + pressure[1, cells + i - shift])
        result[i] = amp[i] * (re * sum_re + im * sum_im)
        return carry

    lax.fori_loop(0, cells, integrate, 0)
    store_2 = pltpu.make_async_copy(result, intensity, store_sem.at[1])
    store_2.start()

    def drain(r, carry):
        for s in (2 * r, 2 * r + 1):
            o_copy(s).wait_send()
            for way in range(2):
                @pl.when(sides[way][1])
                def _():
                    x_copy(s, way).wait_send()

        for way in range(2):
            t_copy(r, 0, way).wait_send()
            t_copy(r, 1, way).wait_send()
            a_copy(r, way).wait_send()

            @pl.when(sides[way][1])
            def _():
                b_copy(r, way).wait_send()
                d_copy(r, way, 0).wait_send()
                d_copy(r, way, 1).wait_send()

        return carry

    lax.fori_loop(0, ROUNDS, drain, 0)
    co_copy().wait_send()
    for way in range(2):
        ct_copy(way).wait_send()

        @pl.when(sides[way][1])
        def _():
            cx_copy(way).wait_send()
            p_copy(way).wait_send()

    store.wait()
    store_2.wait()


def per_device(n_ax, n_az, adjoint, mean_flow, forcing, tke, half_width, start):
    cells, sector, radial = tke.shape
    block = (cells, sector, radial)
    tile = (sector, radial)
    f32 = jnp.float32
    any_spec = pl.BlockSpec(memory_space=pl.ANY)

    def dma(*shape):
        return pltpu.SemaphoreType.DMA(shape)

    def vmem(*shape):
        return pltpu.VMEM(shape, f32)

    return pl.pallas_call(
        functools.partial(kernel, n_ax, n_az),
        out_shape=(
            jax.ShapeDtypeStruct(adjoint.shape, f32),
            jax.ShapeDtypeStruct(tke.shape, f32),
        ),
        in_specs=[pl.BlockSpec(memory_space=pltpu.SMEM)] + [any_spec] * 5,
        out_specs=(any_spec, any_spec),
        scratch_shapes=[
            vmem(3, 5, 2, *block),
            vmem(5, 2, *block),
            vmem(4, *block),
            vmem(2, *block),
            vmem(*block),
            vmem(*block),
            pltpu.VMEM(block, jnp.int32),
            vmem(SEP, *block),
            vmem(3, *block),
            vmem(*block),
            vmem(5, 2, cells + 2, *tile),
            vmem(SECTIONS, 6, *block),
            vmem(ROUNDS, 4, *block),
            vmem(SECTIONS, 2, 5, 2, *tile),
            vmem(SECTIONS, 2, 5, 2, *tile),
            vmem(SECTIONS, 4, *block),
            vmem(SECTIONS, *tile),
            vmem(SECTIONS, *tile),
            vmem(ROUNDS, 2, 10, *tile),
            vmem(ROUNDS, 2, 10, *tile),
            vmem(ROUNDS, *tile),
            vmem(ROUNDS, 2, *tile),
            vmem(ROUNDS, 2, *tile),
            vmem(2, 4, *tile),
            vmem(3, *block),
            vmem(2, *tile),
            vmem(2, *tile),
            vmem(2, 3 * cells, *tile),
            dma(5), dma(2),
            dma(SECTIONS, 2), dma(SECTIONS, 2),
            dma(SECTIONS, 2), dma(SECTIONS, 2),
            dma(SECTIONS), dma(SECTIONS),
            dma(2), dma(2),
            dma(ROUNDS, 2, 2), dma(ROUNDS, 2, 2),
            dma(ROUNDS, 2), dma(ROUNDS, 2),
            dma(ROUNDS, 2), dma(ROUNDS, 2),
            dma(2), dma(2),
            dma(2), dma(2),
            dma(1), dma(1),
        ],
        compiler_params=pltpu.CompilerParams(
            collective_id=0, has_side_effects=True, vmem_limit_bytes=60 * 2**20
        ),
    )(start, adjoint, mean_flow, forcing, tke, half_width)


def solution(mesh):
    return jax.shard_map(
        functools.partial(per_device, mesh.shape["ax"], mesh.shape["az"]),
        mesh=mesh,
        in_specs=(
            P(None, None, "ax", "az", None),
            P(None, "ax", "az", None),
            P(None, "ax", "az", None),
            P("ax", "az", None),
            P("ax", "az", None),
            P(),
        ),
        out_specs=(P(None, None, "ax", "az", None), P("ax", "az", None)),
        check_vma=False,
    )
```

time: 47.7 us -> 41.7 us (0.87)
  Pallas kernels: 43.6 us -> 37.7 us
    pallas_call x1, Pallas kernels: 43.6 us -> 37.7 us  [per_device(): pl.pallas_call(functools.partial(kernel, n_ax, n_az), out_shape=(jax.Shap...]
where the time goes in v2:
time: 41.7 us; the launch traced here: 41.6 us
  Pallas kernels  37.7 us (90%)
  local copies, waits for them, and re-layouts  2.64 us (6%)
  between operations  1.3 us (3%)
    pallas_call x1, Pallas kernels, per_device(): pl.pallas_call(functools.partial(kernel, n_ax, n_az), out_shape=(jax.Shap...  37.7 us
    unnamed x4, local copies, waits for them, and re-layouts  2.64 us

profile of v2, /device:TPU:7, one launch (start us, length us, event | category | flops | bytes accessed | tf_op | source)
XLA Modules:
  0.0 41.6 jit_solution(1314769784111939775)
XLA Ops:
  1.3 37.7 %shard_map.77 = (f32[5,2,16,8,128]{4,3,2,1,0:T(8,128)}, f32[16,8,128]{2,1,0:T(8,128)}) custom-call(s32[1]{0:T(128)S(6)} %copy.10.start, f32[5,2,16,8,128]{4,3,2,1,0:T(8,128)} %adjoint.1, f32[3,16,8,128]{3,2,1,0:T(8,128)} %mean_flow.1, f32[2,16,8,128]{3,2,1,0:T(8,128)} %forcing.1, f32[16,8,128]{2,1,0:T(8,128)} %tke.1, s32[16,8,128]{2,1,0:T(8,128)} %half_width.1), custom_call_target="tpu_custom_call" | custom-call | tf_op jit(solution)/shard_map/pallas_call | solution.py:569
  38.9 0.0 copy-start
  39.0 2.0 %copy.11 = f32[5,2,16,8,128]{4,3,2,1,0:T(8,128)} copy(f32[5,2,16,8,128]{4,3,2,1,0:T(8,128)} %get-tuple-element.4) | data formatting | bytes 1310720
  41.0 0.0 copy-done
  41.0 0.6 %copy.12 = f32[16,8,128]{2,1,0:T(8,128)} copy(f32[16,8,128]{2,1,0:T(8,128)S(1)} %copy-done) | data formatting | bytes 131072
Async XLA Ops:
  38.9 2.0 %copy-start = (f32[16,8,128]{2,1,0:T(8,128)S(1)}, f32[16,8,128]{2,1,0:T(8,128)}, u32[]{:S(2)}) copy-start(f32[16,8,128]{2,1,0:T(8,128)} %get-tuple-element.5) | copy-start | bytes 196612

commit v3 on v2

--- a/solution.py
+++ b/solution.py
@@ -28,7 +28,7 @@
     green, intensity,
     state, partial, coef, force, sigma, amp, width, weights, flow, result,
     flux_x, flux_l, part_l, send_x, recv_x, recv_t, send_o, recv_o,
-    send_d, recv_d, recv_a, send_p, recv_p, coef_x, coef_t, send_c, coef_o, pressure,
+    send_d, recv_d, recv_a, extra_o, send_p, recv_p, coef_x, coef_t, send_c, coef_o, pressure,
     load_sem, store_sem, x_send, x_recv, t_send, t_recv, o_send, o_recv, p_send, p_recv,
     d_send, d_recv, a_send, a_recv, b_send, b_recv, cx_send, cx_recv, ct_send, ct_recv, co_send, co_recv,
 ):
@@ -151,10 +151,12 @@
     def co_copy():
         return remote(send_c, coef_o, co_send.at[0], co_recv.at[0], ax, opposite)
 
-    def p_copy(way):
+    def p_copy(way, piece):
+        first, count = ((1, cells - 2), (0, 1), (cells - 1, 1))[piece]
         return remote(
-            pressure.at[:, pl.ds(cells, cells)], pressure.at[:, pl.ds((0, 2 * cells)[way], cells)],
-            p_send.at[way], p_recv.at[way], sides[way][0], az,
+            pressure.at[:, pl.ds(cells + first, count)],
+            pressure.at[:, pl.ds((0, 2 * cells)[way] + first, count)],
+            p_send.at[way, piece], p_recv.at[way, piece], sides[way][0], az,
         )
 
     def axial(q, u, rho, stiff, inv):
@@ -162,22 +164,23 @@
         return (u * a, rho * a + stiff * e + u * b, u * c, u * d, b * inv + u * e)
 
     def fluxes(s, i, q, gathered):
-        at = pl.ds(i, CHUNK)
+        count = q[0].shape[1]
+        at = pl.ds(i, count)
         u, rho, stiff, inv = coef[0, at], coef[1, at], coef[2, at], coef[3, at]
         a, b, c, d, e = q
         shared = rho * a + stiff * e
         turned, spread = d * inv, c * inv
         along = (u * a, shared + u * b, u * c, u * d, b * inv + u * e)
         for n, f in enumerate(along):
-            flux_x[n, :, pl.ds(i + 1, CHUNK)] = f
+            flux_x[n, :, pl.ds(i + 1, count)] = f
         flux_l[s, 0:2, at] = shared
         flux_l[s, 2:4, at] = turned
         flux_l[s, 4:6, at] = spread
         if gathered is None:
             return None
         r = s // 2
-        for way, end, k in ((1, 0, 0), (0, cells - CHUNK, CHUNK - 1)):
-            if i == end:
+        for way, k in ((1, -i), (0, cells - 1 - i)):
+            if 0 <= k < count:
                 for n, f in enumerate(along):
                     send_x[s, way, n] = f[:, k]
                 for n, f in enumerate((along[0], along[3], along[4], shared, turned)):
@@ -189,7 +192,7 @@
                 send_p[r, way] = packed
         for n, f in enumerate((shared, spread, turned)):
             for part in range(2):
-                for k in range(CHUNK):
+                for k in range(count):
                     gathered[n] = lane_pack(lane, gathered[n], f[part, k], (2 * n + part) * cells + i + k)
         return gathered
 
@@ -253,30 +256,27 @@
         source = lax.rem(s, 3)
         scale = weight_of(s) * tau
 
-        def body(t, carry):
-            i = t * CHUNK
+        half = 0.5 * scale
+        turned_by = scale * FREQUENCY
+
+        def radially(f):
+            return outward * pltpu.roll(f, radial - 1, 3) - inward * pltpu.roll(f, 1, 3)
+
+        def around(f):
+            return up * pltpu.roll(f, sector - 1, 2) - down * pltpu.roll(f, 1, 2)
+
+        for i in range(0, cells, CHUNK):
             at = pl.ds(i, CHUNK)
-            damp = sigma[at]
+            fade = scale * sigma[at]
             shared, turned, spread = flux_l[s, 0:2, at], flux_l[s, 2:4, at], flux_l[s, 4:6, at]
-
-            def radially(f):
-                return outward * pltpu.roll(f, radial - 1, 3) - inward * pltpu.roll(f, 1, 3)
-
-            def around(f):
-                return up * pltpu.roll(f, sector - 1, 2) - down * pltpu.roll(f, 1, 2)
-
             extra = (None, None, radially(shared), around(shared), radially(spread) + around(turned) + force[:, at])
             for n in range(5):
                 q = state[source, n, :, at]
-                total = 0.5 * (flux_x[n, :, pl.ds(i + 2, CHUNK)] - flux_x[n, :, at]) - damp * q
+                total = state[0, n, :, at] + half * (flux_x[n, :, pl.ds(i + 2, CHUNK)] - flux_x[n, :, at]) - fade * q
                 if extra[n] is not None:
-                    total = total + extra[n]
-                base = state[0, n, :, at]
-                partial[n, 0, at] = base[0] + scale * (total[0] + FREQUENCY * q[1])
-                partial[n, 1, at] = base[1] + scale * (total[1] - FREQUENCY * q[0])
-            return carry
-
-        lax.fori_loop(0, cells // CHUNK, body, 0)
+                    total = total + scale * extra[n]
+                partial[n, 0, at] = total[0] + turned_by * q[1]
+                partial[n, 1, at] = total[1] - turned_by * q[0]
 
     def receive(r, later):
         s = 2 * r + later
@@ -290,12 +290,11 @@
         o_copy(s).wait_recv()
 
     def complete(r):
-        s = 2 * r + 1
-        scale = weight_of(2 * r) * tau
-        half = 0.5 * scale
-        scale_0 = weight_of(2 * r) * tau_0
-        half_0 = 0.5 * scale_0
+        scale, scale_0 = weight_of(2 * r) * tau, weight_of(2 * r) * tau_0
+        half, half_0 = 0.5 * scale, 0.5 * scale_0
         around = scale * edge
+        scale_2 = weight_of(2 * r + 1) * tau
+        rows = scale_2 * edge
         a_copy(r, 0).wait_recv()
         a_copy(r, 1).wait_recv()
         aside = jnp.where(is_edge, recv_a[r], 0.0)
@@ -316,18 +315,16 @@
             )
             more_d = -around * flux_l[2 * r, 0:2, at]
             more_e = spun - around * flux_l[2 * r, 2:4, at]
-            recv_t[s, 0:2, at] = recv_t[s, 0:2, at] + coef_t[1, at] * more_e
-            recv_t[s, 2:4, at] = recv_t[s, 2:4, at] + coef_t[2, at] * more_d
+            partial[3, :, at] = partial[3, :, at] + rows * jnp.where(is_edge, coef_t[1, at] * more_e, 0.0)
+            partial[4, :, at] = partial[4, :, at] + rows * jnp.where(is_edge, coef_t[2, at] * more_d, 0.0)
 
         mine = send_o[2 * r]
         more_c = -half_0 * pltpu.roll(mine, 2 * cells, 1)
         more_e = -half_0 * pltpu.roll(mine, radial - 2 * cells, 1) + scale_0 * edge_0 * pltpu.roll(
             aside, radial - 4 * cells, 1
         )
-        recv_o[s] = (
-            recv_o[s]
-            + coef_o[0] * jnp.where(lane < 2 * cells, 0.0, more_c)
-            + coef_o[1] * jnp.where(lane < 2 * cells, more_e, 0.0)
+        extra_o[...] = coef_o[0] * jnp.where(lane < 2 * cells, 0.0, more_c) + coef_o[1] * jnp.where(
+            lane < 2 * cells, more_e, 0.0
         )
 
         for way, i, sign in ((0, 0, 1.0), (1, cells - 1, -1.0)):
@@ -337,10 +334,26 @@
                 d_copy(r, way, 1).wait_recv()
                 corner = jnp.where(is_edge, recv_d[r, way], 0.0)
                 gone = (-sign * half) * corner[0:6]
-                recv_t[s, 0:2, i] = recv_t[s, 0:2, i] + coef_t[0, i] * gone[0:2] + coef_t[1, i] * gone[4:6]
-                recv_t[s, 2:4, i] = recv_t[s, 2:4, i] + coef_t[2, i] * gone[2:4]
+                more = [(sign * half) * send_x[2 * r, 1 - way, n] for n in range(5)]
+                more[3] = more[3] + around * corner[6:8]
+                more[4] = more[4] + around * corner[8:10]
+                c = coef_x[way]
+                along = axial(more, c[0], c[1], c[2], c[3])
+                turned = [None, None, None]
+                turned += [rows * jnp.where(is_edge, coef_t[0, i] * gone[0:2] + coef_t[1, i] * gone[4:6], 0.0)]
+                turned += [rows * jnp.where(is_edge, coef_t[2, i] * gone[2:4], 0.0)]
+                for n in range(5):
+                    q = partial[n, :, i] - (0.5 * sign * scale_2) * along[n]
+                    partial[n, :, i] = q if turned[n] is None else q + turned[n]
+
+    def complete_ends(r):
+        half_0 = (0.5 * tau_0) * weight_of(2 * r)
+        half = (0.5 * weight_of(2 * r + 1)) * tau
+        for way, i, sign in ((0, 0, 1.0), (1, cells - 1, -1.0)):
+            @pl.when(sides[1 - way][1])
+            def _():
                 b_copy(r, way).wait_recv()
-                packed = recv_p[r, way]
+                packed = -half_0 * recv_p[r, way]
 
                 def at_axis(n):
                     return jnp.stack(
@@ -350,37 +363,36 @@
                         ]
                     )
 
-                more = [(sign * half) * send_x[2 * r, 1 - way, n] for n in range(5)]
-                more[2] = more[2] - half * at_axis(0)
-                more[3] = more[3] + around * corner[6:8]
-                more[4] = more[4] + around * corner[8:10] - half * at_axis(2)
-                c = coef_x[way]
-                for n, f in enumerate(axial(more, c[0], c[1], c[2], c[3])):
-                    recv_x[s, way, n] = recv_x[s, way, n] + f
+                c, e = (-sign * half) * at_axis(0), (-sign * half) * at_axis(2)
+                u, stiff = coef_x[way, 0], coef_x[way, 2]
+                partial[1, :, i] = partial[1, :, i] + stiff * e
+                partial[2, :, i] = partial[2, :, i] + u * c
+                partial[4, :, i] = partial[4, :, i] + u * e
 
                 def spread_out(n, to):
                     low = pltpu.roll(packed, (radial + to + i - n) % radial, 1)
                     high = pltpu.roll(packed, (radial + to + cells + i - n - 1) % radial, 1)
                     return jnp.where(lane == to + i, low, jnp.where(lane == to + cells + i, high, 0.0))
 
-                recv_o[s] = recv_o[s] - (sign * half_0) * (
+                extra_o[...] = extra_o[...] + sign * (
                     coef_o[0] * (spread_out(4, 0) + spread_out(6, 2 * cells)) + coef_o[1] * spread_out(8, 0)
                 )
 
-    def outer(s, then):
-        scale = weight_of(s) * tau
-        half = 0.5 * scale
+    def add_x(s):
+        half = (0.5 * weight_of(s)) * tau
         for way, i, sign in ((0, 0, -1.0), (1, cells - 1, 1.0)):
             @pl.when(sides[1 - way][1])
             def _():
                 partial[:, :, i] = partial[:, :, i] + (sign * half) * recv_x[s, way]
 
+    def outer(s, chunks, then, gathered=None):
+        scale = weight_of(s) * tau
         rows = scale * edge
-        mirror = (-0.5 * tau_0) * weight_of(s) * recv_o[s]
+        mirror = recv_o[s] if then == "plain" else recv_o[s] + extra_o[...]
+        mirror = (-0.5 * tau_0) * weight_of(s) * mirror
         target = lax.rem(s + 1, 3)
-        gathered = nothing(3) if then == "round" else None
-        for i in range(0, cells, CHUNK):
-            at = pl.ds(i, CHUNK)
+        for i, count in chunks:
+            at = pl.ds(i, count)
             q = [partial[n, :, at] for n in range(5)]
             ring = jnp.where(is_edge, recv_t[s, :, at], 0.0) * rows
             spun = [
@@ -389,7 +401,7 @@
                         jnp.stack(
                             [
                                 jnp.where(is_axis, pltpu.roll(mirror, (radial - n * cells - i - k) % radial, 1), 0.0)
-                                for k in range(CHUNK)
+                                for k in range(count)
                             ]
                         )
                         for n in (c, c + 1)
@@ -403,11 +415,10 @@
             for n in range(5):
                 state[target, n, :, at] = q[n]
             if then == "none":
-                pressure[:, pl.ds(cells + i, CHUNK)] = q[4]
+                pressure[:, pl.ds(cells + i, count)] = q[4]
             else:
                 gathered = fluxes(s + 1, i, q, gathered)
-        if then == "round":
-            join(s + 1, gathered)
+        return gathered
 
     def join(s, gathered):
         send_o[s] = jnp.where(lane < 2 * cells, gathered[0], jnp.where(lane < 4 * cells, gathered[1], gathered[2]))
@@ -444,14 +455,17 @@
             cx_copy(way).start()
 
     loads[2].wait()
+    whole = [(i, CHUNK) for i in range(0, cells, CHUNK)]
+    middle = [(i, min(CHUNK, cells - 1 - i)) for i in range(1, cells - 1, CHUNK)]
+    ends = [(0, 1), (cells - 1, 1)]
 
     def first_half(r):
         inner(2 * r)
         known(r)
         receive(r, 0)
-        outer(2 * r, "plain")
+        add_x(2 * r)
+        outer(2 * r, whole, "plain")
         inner(2 * r + 1)
-        receive(r, 1)
 
     def round_(r, carry):
         first_half(r)
@@ -467,7 +481,12 @@
                     cx_copy(way).wait_recv()
 
         complete(r)
-        outer(2 * r + 1, "round")
+        receive(r, 1)
+        add_x(2 * r + 1)
+        gathered = outer(2 * r + 1, middle, "round", nothing(3))
+        complete_ends(r)
+        gathered = outer(2 * r + 1, ends, "round", gathered)
+        join(2 * r + 2, gathered)
         send(r + 1)
 
         @pl.when(r == 0)
@@ -489,12 +508,21 @@
     last = ROUNDS - 1
     first_half(last)
     complete(last)
-    outer(2 * last + 1, "none")
-
+    receive(last, 1)
+    add_x(2 * last + 1)
+    outer(2 * last + 1, middle, "none")
     for way in range(2):
         @pl.when(sides[way][1])
         def _():
-            p_copy(way).start()
+            p_copy(way, 0).start()
+
+    complete_ends(last)
+    outer(2 * last + 1, ends, "none")
+    for way in range(2):
+        @pl.when(sides[way][1])
+        def _():
+            p_copy(way, 1).start()
+            p_copy(way, 2).start()
 
     store = pltpu.make_async_copy(state.at[0], green, store_sem.at[0])
     store.start()
@@ -502,7 +530,8 @@
     for way in range(2):
         @pl.when(sides[1 - way][1])
         def _():
-            p_copy(way).wait_recv()
+            for piece in range(3):
+                p_copy(way, piece).wait_recv()
 
     def integrate(i, carry):
         re, im = pressure[0, cells + i], pressure[1, cells + i]
@@ -547,10 +576,24 @@
         @pl.when(sides[way][1])
         def _():
             cx_copy(way).wait_send()
-            p_copy(way).wait_send()
+            for piece in range(3):
+                p_copy(way, piece).wait_send()
 
     store.wait()
     store_2.wait()
+
+
+def hand_over(green, intensity, green_out, intensity_out, held, held_2, load_sem, store_sem):
+    parts = [(green.at[n], held.at[n], green_out.at[n]) for n in range(5)] + [(intensity, held_2, intensity_out)]
+    loads = [pltpu.make_async_copy(src, mid, load_sem.at[n]) for n, (src, mid, _) in enumerate(parts)]
+    stores = [pltpu.make_async_copy(mid, dst, store_sem.at[n]) for n, (_, mid, dst) in enumerate(parts)]
+    for load in loads:
+        load.start()
+    for load, store in zip(loads, stores):
+        load.wait()
+        store.start()
+    for store in stores:
+        store.wait()
 
 
 def per_device(n_ax, n_az, adjoint, mean_flow, forcing, tke, half_width, start):
@@ -566,7 +609,7 @@
     def vmem(*shape):
         return pltpu.VMEM(shape, f32)
 
-    return pl.pallas_call(
+    results = pl.pallas_call(
         functools.partial(kernel, n_ax, n_az),
         out_shape=(
             jax.ShapeDtypeStruct(adjoint.shape, f32),
@@ -596,6 +639,7 @@
             vmem(ROUNDS, 2, 10, *tile),
             vmem(ROUNDS, 2, 10, *tile),
             vmem(ROUNDS, *tile),
+            vmem(*tile),
             vmem(ROUNDS, 2, *tile),
             vmem(ROUNDS, 2, *tile),
             vmem(2, 4, *tile),
@@ -607,7 +651,7 @@
             dma(SECTIONS, 2), dma(SECTIONS, 2),
             dma(SECTIONS, 2), dma(SECTIONS, 2),
             dma(SECTIONS), dma(SECTIONS),
-            dma(2), dma(2),
+            dma(2, 3), dma(2, 3),
             dma(ROUNDS, 2, 2), dma(ROUNDS, 2, 2),
             dma(ROUNDS, 2), dma(ROUNDS, 2),
             dma(ROUNDS, 2), dma(ROUNDS, 2),
@@ -619,6 +663,17 @@
             collective_id=0, has_side_effects=True, vmem_limit_bytes=60 * 2**20
         ),
     )(start, adjoint, mean_flow, forcing, tke, half_width)
+    return pl.pallas_call(
+        hand_over,
+        out_shape=(
+            jax.ShapeDtypeStruct(adjoint.shape, f32),
+            jax.ShapeDtypeStruct(tke.shape, f32),
+        ),
+        in_specs=[any_spec] * 2,
+        out_specs=(any_spec, any_spec),
+        scratch_shapes=[vmem(5, 2, *block), vmem(*block), dma(6), dma(6)],
+        compiler_params=pltpu.CompilerParams(vmem_limit_bytes=60 * 2**20),
+    )(*results)
 
 
 def solution(mesh):

time: 41.7 us -> 39.9 us (0.957)
  local copies, waits for them, and re-layouts: 2.64 us -> 0 us
  Pallas kernels: 37.7 us -> 38.5 us
    unnamed x4 -> x0, local copies, waits for them, and re-layouts: 2.64 us -> none
    pallas_call x0 -> x1, Pallas kernels: none -> 1.94 us  [per_device(): pl.pallas_call(hand_over, out_shape=(jax.ShapeDtypeStruct(adjoint.shape,...]
    pallas_call x1, Pallas kernels: 37.7 us -> 36.6 us  [per_device(): pl.pallas_call(functools.partial(kernel, n_ax, n_az), out_shape=(jax.Shap...]
where the time goes in v3:
time: 39.9 us; the launch traced here: 39.8 us
  Pallas kernels  38.5 us (96%)
  between operations  1.29 us (3%)
    pallas_call x1, Pallas kernels, per_device(): pl.pallas_call(functools.partial(kernel, n_ax, n_az), out_shape=(jax.Shap...  36.6 us
    pallas_call x1, Pallas kernels, per_device(): pl.pallas_call(hand_over, out_shape=(jax.ShapeDtypeStruct(adjoint.shape,...  1.94 us

profile of v3, /device:TPU:7, one launch (start us, length us, event | category | flops | bytes accessed | tf_op | source)
XLA Modules:
  0.0 39.8 jit_solution(16179748950441617312)
XLA Ops:
  1.3 36.6 %shard_map.77 = (f32[5,2,16,8,128]{4,3,2,1,0:T(8,128)}, f32[16,8,128]{2,1,0:T(8,128)}) custom-call(s32[1]{0:T(128)S(6)} %copy.8.start, f32[5,2,16,8,128]{4,3,2,1,0:T(8,128)} %adjoint.1, f32[3,16,8,128]{3,2,1,0:T(8,128)} %mean_flow.1, f32[2,16,8,128]{3,2,1,0:T(8,128)} %forcing.1, f32[16,8,128]{2,1,0:T(8,128)} %tke.1, s32[16,8,128]{2,1,0:T(8,128)} %half_width.1), custom_call_target="tpu_custom_call" | custom-call | tf_op jit(solution)/shard_map/pallas_call | solution.py:612
  37.8 1.9 %shard_map.78 = (f32[5,2,16,8,128]{4,3,2,1,0:T(8,128)}, f32[16,8,128]{2,1,0:T(8,128)}) custom-call(f32[5,2,16,8,128]{4,3,2,1,0:T(8,128)} %get-tuple-element.4.green, f32[16,8,128]{2,1,0:T(8,128)} %get-tuple-element.5.intensity), custom_call_target="tpu_custom_call" | custom-call | tf_op jit(solution)/shard_map/pallas_call | solution.py:666

commit v4 on v3

--- a/solution.py
+++ b/solution.py
@@ -25,13 +25,16 @@
 def kernel(
     n_ax, n_az,
     start, adjoint, mean_flow, forcing, tke, half_width,
-    green, intensity,
-    state, partial, coef, force, sigma, amp, width, weights, flow, result,
-    flux_x, flux_l, part_l, send_x, recv_x, recv_t, send_o, recv_o,
-    send_d, recv_d, recv_a, extra_o, send_p, recv_p, coef_x, coef_t, send_c, coef_o, pressure,
-    load_sem, store_sem, x_send, x_recv, t_send, t_recv, o_send, o_recv, p_send, p_recv,
-    d_send, d_recv, a_send, a_recv, b_send, b_recv, cx_send, cx_recv, ct_send, ct_recv, co_send, co_recv,
+    *refs,
 ):
+    green, intensity = refs[:10], refs[10]
+    (
+        state, partial, coef, force, sigma, amp, width, weights, flow, result,
+        flux_x, flux_l, part_l, send_x, recv_x, recv_t, send_o, recv_o,
+        send_d, recv_d, recv_a, extra_o, send_p, recv_p, coef_x, coef_t, send_c, coef_o, pressure,
+        load_sem, store_sem, x_send, x_recv, t_send, t_recv, o_send, o_recv, p_send, p_recv,
+        d_send, d_recv, a_send, a_recv, b_send, b_recv, cx_send, cx_recv, ct_send, ct_recv, co_send, co_recv,
+    ) = refs[11:]
     cells, sector, radial = state.shape[3], state.shape[4], state.shape[5]
     ax, az = lax.axis_index("ax"), lax.axis_index("az")
     half_turn = n_az // 2
@@ -524,8 +527,9 @@
             p_copy(way, 1).start()
             p_copy(way, 2).start()
 
-    store = pltpu.make_async_copy(state.at[0], green, store_sem.at[0])
-    store.start()
+    stores = [pltpu.make_async_copy(state.at[0, n // 2, n % 2], green[n], store_sem.at[n]) for n in range(10)]
+    for store in stores:
+        store.start()
     loads[4].wait()
     for way in range(2):
         @pl.when(sides[1 - way][1])
@@ -544,8 +548,8 @@
         return carry
 
     lax.fori_loop(0, cells, integrate, 0)
-    store_2 = pltpu.make_async_copy(result, intensity, store_sem.at[1])
-    store_2.start()
+    stores.append(pltpu.make_async_copy(result, intensity, store_sem.at[10]))
+    stores[10].start()
 
     def drain(r, carry):
         for s in (2 * r, 2 * r + 1):
@@ -579,21 +583,18 @@
             for piece in range(3):
                 p_copy(way, piece).wait_send()
 
-    store.wait()
-    store_2.wait()
-
-
-def hand_over(green, intensity, green_out, intensity_out, held, held_2, load_sem, store_sem):
-    parts = [(green.at[n], held.at[n], green_out.at[n]) for n in range(5)] + [(intensity, held_2, intensity_out)]
-    loads = [pltpu.make_async_copy(src, mid, load_sem.at[n]) for n, (src, mid, _) in enumerate(parts)]
-    stores = [pltpu.make_async_copy(mid, dst, store_sem.at[n]) for n, (_, mid, dst) in enumerate(parts)]
-    for load in loads:
-        load.start()
-    for load, store in zip(loads, stores):
-        load.wait()
-        store.start()
     for store in stores:
         store.wait()
+
+
+def hand_over(*refs):
+    fields, (green, intensity, sem) = refs[:11], refs[11:]
+    places = [green.at[n // 2, n % 2] for n in range(10)] + [intensity]
+    copies = [pltpu.make_async_copy(src, dst, sem.at[n]) for n, (src, dst) in enumerate(zip(fields, places))]
+    for copy in copies:
+        copy.start()
+    for copy in copies:
+        copy.wait()
 
 
 def per_device(n_ax, n_az, adjoint, mean_flow, forcing, tke, half_width, start):
@@ -611,12 +612,9 @@
 
     results = pl.pallas_call(
         functools.partial(kernel, n_ax, n_az),
-        out_shape=(
-            jax.ShapeDtypeStruct(adjoint.shape, f32),
-            jax.ShapeDtypeStruct(tke.shape, f32),
-        ),
+        out_shape=[jax.ShapeDtypeStruct(block, f32)] * 11,
         in_specs=[pl.BlockSpec(memory_space=pltpu.SMEM)] + [any_spec] * 5,
-        out_specs=(any_spec, any_spec),
+        out_specs=[any_spec] * 11,
         scratch_shapes=[
             vmem(3, 5, 2, *block),
             vmem(5, 2, *block),
@@ -647,7 +645,7 @@
             vmem(2, *tile),
             vmem(2, *tile),
             vmem(2, 3 * cells, *tile),
-            dma(5), dma(2),
+            dma(5), dma(11),
             dma(SECTIONS, 2), dma(SECTIONS, 2),
             dma(SECTIONS, 2), dma(SECTIONS, 2),
             dma(SECTIONS), dma(SECTIONS),
@@ -660,7 +658,7 @@
             dma(1), dma(1),
         ],
         compiler_params=pltpu.CompilerParams(
-            collective_id=0, has_side_effects=True, vmem_limit_bytes=60 * 2**20
+            collective_id=0, has_side_effects=True, vmem_limit_bytes=54528 * 1024
         ),
     )(start, adjoint, mean_flow, forcing, tke, half_width)
     return pl.pallas_call(
@@ -669,10 +667,10 @@
             jax.ShapeDtypeStruct(adjoint.shape, f32),
             jax.ShapeDtypeStruct(tke.shape, f32),
         ),
-        in_specs=[any_spec] * 2,
+        in_specs=[any_spec] * 11,
         out_specs=(any_spec, any_spec),
-        scratch_shapes=[vmem(5, 2, *block), vmem(*block), dma(6), dma(6)],
-        compiler_params=pltpu.CompilerParams(vmem_limit_bytes=60 * 2**20),
+        scratch_shapes=[dma(11)],
+        compiler_params=pltpu.CompilerParams(vmem_limit_bytes=2**20),
     )(*results)
 
 

time: 39.9 us -> 38.6 us (0.967)
  Pallas kernels: 38.5 us -> 37.2 us
    pallas_call x1, Pallas kernels: 1.94 us -> 0.94 us  [per_device(): pl.pallas_call(hand_over, out_shape=(jax.ShapeDtypeStruct(adjoint.shape,...]
where the time goes in v4:
time: 38.6 us; the launch traced here: 38.5 us
  Pallas kernels  37.2 us (96%)
  between operations  1.29 us (3%)
    pallas_call x1, Pallas kernels, per_device(): pl.pallas_call(functools.partial(kernel, n_ax, n_az), out_shape=[jax.Shap...  36.2 us
    pallas_call x1, Pallas kernels, per_device(): pl.pallas_call(hand_over, out_shape=(jax.ShapeDtypeStruct(adjoint.shape,...  0.94 us

profile of v4, /device:TPU:7, one launch (start us, length us, event | category | flops | bytes accessed | tf_op | source)
XLA Modules:
  0.0 38.5 jit_solution(8856574880003219668)
XLA Ops:
  1.3 36.2 %shard_map.77 = (f32[16,8,128]{2,1,0:T(8,128)S(1)}, f32[16,8,128]{2,1,0:T(8,128)S(1)}, f32[16,8,128]{2,1,0:T(8,128)S(1)}, f32[16,8,128]{2,1,0:T(8,128)S(1)}, f32...) custom-call(s32[1]{0:T(128)S(6)} %copy.8.start, ...), custom_call_target="tpu_custom_call" | custom-call | tf_op jit(solution)/shard_map/pallas_call | solution.py:613
  37.5 0.9 %shard_map.78 = (f32[5,2,16,8,128]{4,3,2,1,0:T(8,128)}, f32[16,8,128]{2,1,0:T(8,128)}) custom-call(f32[16,8,128]{2,1,0:T(8,128)S(1)} %get-tuple-element.13.refs_0_, f32[16,8,128]{2,1,0:T(8,128)S(1)} %get-tuple-element.14.refs_1_, f32[16,8,128]{2,1,0:T(8,128)S(1)} %get-tuple-element.15.refs_2_, f32[16,8,128]{2,1,0:T(8,128)S(1)} %get-tuple-element.16.refs_3_, ...), custom_call_target="tpu_custom_call" | custom-call | tf_op jit(solution)/shard_map/pallas_call | solution.py:664

commit v5 on v4

--- a/solution.py
+++ b/solution.py
@@ -530,27 +530,6 @@
     stores = [pltpu.make_async_copy(state.at[0, n // 2, n % 2], green[n], store_sem.at[n]) for n in range(10)]
     for store in stores:
         store.start()
-    loads[4].wait()
-    for way in range(2):
-        @pl.when(sides[1 - way][1])
-        def _():
-            for piece in range(3):
-                p_copy(way, piece).wait_recv()
-
-    def integrate(i, carry):
-        re, im = pressure[0, cells + i], pressure[1, cells + i]
-        sum_re, sum_im = re, im
-        for shift in range(1, SEP + 1):
-            w = weights[shift - 1, i]
-            sum_re = sum_re + w * (pressure[0, cells + i + shift] + pressure[0, cells + i - shift])
-            sum_im = sum_im + w * (pressure[1, cells + i + shift] + pressure[1, cells + i - shift])
-        result[i] = amp[i] * (re * sum_re + im * sum_im)
-        return carry
-
-    lax.fori_loop(0, cells, integrate, 0)
-    stores.append(pltpu.make_async_copy(result, intensity, store_sem.at[10]))
-    stores[10].start()
-
     def drain(r, carry):
         for s in (2 * r, 2 * r + 1):
             o_copy(s).wait_send()
@@ -580,11 +559,37 @@
         @pl.when(sides[way][1])
         def _():
             cx_copy(way).wait_send()
+
+    for store in stores:
+        store.wait()
+
+    loads[4].wait()
+    for way in range(2):
+        @pl.when(sides[1 - way][1])
+        def _():
+            for piece in range(3):
+                p_copy(way, piece).wait_recv()
+
+    for i in range(0, cells, CHUNK):
+        re, im = (pressure[part, pl.ds(cells + i, CHUNK)] for part in range(2))
+        sum_re, sum_im = re, im
+        for shift in range(1, SEP + 1):
+            w = weights[shift - 1, pl.ds(i, CHUNK)]
+            ahead, behind = pl.ds(cells + i + shift, CHUNK), pl.ds(cells + i - shift, CHUNK)
+            sum_re = sum_re + w * (pressure[0, ahead] + pressure[0, behind])
+            sum_im = sum_im + w * (pressure[1, ahead] + pressure[1, behind])
+        result[pl.ds(i, CHUNK)] = amp[pl.ds(i, CHUNK)] * (re * sum_re + im * sum_im)
+
+    last_store = pltpu.make_async_copy(result, intensity, store_sem.at[10])
+    last_store.start()
+
+    for way in range(2):
+        @pl.when(sides[way][1])
+        def _():
             for piece in range(3):
                 p_copy(way, piece).wait_send()
 
-    for store in stores:
-        store.wait()
+    last_store.wait()
 
 
 def hand_over(*refs):

time: 38.6 us -> 38.3 us (level)
  no operation moved by 1% of the time
where the time goes in v5:
time: 38.3 us; the launch traced here: 38.2 us
  Pallas kernels  36.9 us (96%)
  between operations  1.29 us (3%)
    pallas_call x1, Pallas kernels, per_device(): pl.pallas_call(functools.partial(kernel, n_ax, n_az), out_shape=[jax.Shap...  36 us
    pallas_call x1, Pallas kernels, per_device(): pl.pallas_call(hand_over, out_shape=(jax.ShapeDtypeStruct(adjoint.shape,...  0.94 us

profile of v5, /device:TPU:7, one launch (start us, length us, event | category | flops | bytes accessed | tf_op | source)
XLA Modules:
  0.0 38.2 jit_solution(6581877883087673260)
XLA Ops:
  1.3 36.0 %shard_map.77 = (f32[16,8,128]{2,1,0:T(8,128)S(1)}, f32[16,8,128]{2,1,0:T(8,128)S(1)}, f32[16,8,128]{2,1,0:T(8,128)S(1)}, f32[16,8,128]{2,1,0:T(8,128)S(1)}, f32...) custom-call(s32[1]{0:T(128)S(6)} %copy.8.start, ...), custom_call_target="tpu_custom_call" | custom-call | tf_op jit(solution)/shard_map/pallas_call | solution.py:618
  37.2 0.9 %shard_map.78 = (f32[5,2,16,8,128]{4,3,2,1,0:T(8,128)}, f32[16,8,128]{2,1,0:T(8,128)}) custom-call(f32[16,8,128]{2,1,0:T(8,128)S(1)} %get-tuple-element.13.refs_0_, f32[16,8,128]{2,1,0:T(8,128)S(1)} %get-tuple-element.14.refs_1_, f32[16,8,128]{2,1,0:T(8,128)S(1)} %get-tuple-element.15.refs_2_, f32[16,8,128]{2,1,0:T(8,128)S(1)} %get-tuple-element.16.refs_3_, ...), custom_call_target="tpu_custom_call" | custom-call | tf_op jit(solution)/shard_map/pallas_call | solution.py:669

commit v6 on v5

--- a/solution.py
+++ b/solution.py
@@ -462,16 +462,30 @@
     middle = [(i, min(CHUNK, cells - 1 - i)) for i in range(1, cells - 1, CHUNK)]
     ends = [(0, 1), (cells - 1, 1)]
 
-    def first_half(r):
+    def first_half(r, weighs):
         inner(2 * r)
         known(r)
+        if weighs:
+            @pl.when(r == 0)
+            def _():
+                loads[3].wait()
+
+                def weigh(i, carry):
+                    length = width[i].astype(jnp.float32)
+                    inverse = 1.0 / (length * length)
+                    for shift in range(1, SEP + 1):
+                        weights[shift - 1, i] = jnp.exp(-(shift * shift) * inverse)
+                    return carry
+
+                lax.fori_loop(0, cells, weigh, 0)
+
         receive(r, 0)
         add_x(2 * r)
         outer(2 * r, whole, "plain")
         inner(2 * r + 1)
 
     def round_(r, carry):
-        first_half(r)
+        first_half(r, True)
 
         @pl.when(r == 0)
         def _():
@@ -492,24 +506,11 @@
         join(2 * r + 2, gathered)
         send(r + 1)
 
-        @pl.when(r == 0)
-        def _():
-            loads[3].wait()
-
-            def weigh(i, carry):
-                length = width[i].astype(jnp.float32)
-                inverse = 1.0 / (length * length)
-                for shift in range(1, SEP + 1):
-                    weights[shift - 1, i] = jnp.exp(-(shift * shift) * inverse)
-                return carry
-
-            lax.fori_loop(0, cells, weigh, 0)
-
         return carry
 
     lax.fori_loop(0, ROUNDS - 1, round_, 0)
     last = ROUNDS - 1
-    first_half(last)
+    first_half(last, False)
     complete(last)
     receive(last, 1)
     add_x(2 * last + 1)

time: 38.3 us -> 38.1 us (level)
  no operation moved by 1% of the time
where the time goes in v6:
time: 38.1 us; the launch traced here: 38 us
  Pallas kernels  36.7 us (96%)
  between operations  1.29 us (3%)
    pallas_call x1, Pallas kernels, per_device(): pl.pallas_call(functools.partial(kernel, n_ax, n_az), out_shape=[jax.Shap...  35.8 us
    pallas_call x1, Pallas kernels, per_device(): pl.pallas_call(hand_over, out_shape=(jax.ShapeDtypeStruct(adjoint.shape,...  0.94 us

profile of v6, /device:TPU:7, one launch (start us, length us, event | category | flops | bytes accessed | tf_op | source)
XLA Modules:
  0.0 38.0 jit_solution(14900240495170107651)
XLA Ops:
  1.3 35.8 %shard_map.77 = (f32[16,8,128]{2,1,0:T(8,128)S(1)}, f32[16,8,128]{2,1,0:T(8,128)S(1)}, f32[16,8,128]{2,1,0:T(8,128)S(1)}, f32[16,8,128]{2,1,0:T(8,128)S(1)}, f32...) custom-call(s32[1]{0:T(128)S(6)} %copy.8.start, ...), custom_call_target="tpu_custom_call" | custom-call | tf_op jit(solution)/shard_map/pallas_call | solution.py:619
  37.1 0.9 %shard_map.78 = (f32[5,2,16,8,128]{4,3,2,1,0:T(8,128)}, f32[16,8,128]{2,1,0:T(8,128)}) custom-call(f32[16,8,128]{2,1,0:T(8,128)S(1)} %get-tuple-element.13.refs_0_, f32[16,8,128]{2,1,0:T(8,128)S(1)} %get-tuple-element.14.refs_1_, f32[16,8,128]{2,1,0:T(8,128)S(1)} %get-tuple-element.15.refs_2_, f32[16,8,128]{2,1,0:T(8,128)S(1)} %get-tuple-element.16.refs_3_, ...), custom_call_target="tpu_custom_call" | custom-call | tf_op jit(solution)/shard_map/pallas_call | solution.py:670
